TPU v7x, 128 devices: a whole 4x4x4 slice. The times are simulated.
128 devices in a mesh: lon: 16 (over y, z_hi, core), lat: 8 (over z_lo, x).
Axes of the slice: x: 4, y: 4, z: 4 (z_hi: 2, z_lo: 2; z = z_hi * 2 + z_lo), core: 2. Of those that a mesh axis runs over, the one named last changes fastest.
Arguments:
- tokens: bfloat16 [2, 48, 768, 192], P(None, 'lat', 'lon'), may hold values from -80 to 80
- cotangent: bfloat16 [2, 48, 768, 192], P(None, 'lat', 'lon'), may hold values from -6 to 6
- ln1_gain: float32 [192], replicated, may hold values from 0.1 to 1.9
- w_qkv: bfloat16 [192, 576], replicated, may hold values from -0.4375 to 0.4375
- w_proj: bfloat16 [192, 192], replicated, may hold values from -0.4375 to 0.4375
- ln2_gain: float32 [192], replicated, may hold values from 0.1 to 1.9
- w_up: bfloat16 [192, 768], replicated, may hold values from -0.4375 to 0.4375
- w_down: bfloat16 [768, 192], replicated, may hold values from -0.21875 to 0.21875
- bias_table: float32 [8, 6, 3312], P('lat'), may hold values from -4 to 402
Outputs:
- d_tokens: bfloat16 [2, 48, 768, 192], P(None, 'lat', 'lon')
- d_ln1_gain: float32 [192], replicated
- d_w_qkv: float32 [192, 576], replicated
- d_w_proj: float32 [192, 192], replicated
- d_ln2_gain: float32 [192], replicated
- d_w_up: float32 [192, 768], replicated
- d_w_down: float32 [768, 192], replicated
- d_bias_table: float32 [8, 6, 3312], P('lat')
All inputs are finite; a program needn't handle non-finite values.
Results may differ from a plain program's by a relative error of at most 0.019.
Values may be sent and summed in bfloat16 or wider, within the bound.
No kernel may reach another device: no remote copies, remote signals or barrier semaphores. Data moves between devices by JAX's collectives and lax.ppermute only.
A program may use at most 128 MiB of HBM per device.

v0:
```python
import functools
import math

import jax
import jax.numpy as jnp
from jax import lax
from jax.experimental import pallas as pl
from jax.experimental.pallas import tpu as pltpu
from jax.sharding import Mesh
from jax.sharding import PartitionSpec as P

BF = jnp.bfloat16
F32 = jnp.float32
D = 192
HEADS = 6
DH = 32
MLP = 768
WIN_LAT = 6
WIN_LON = 12
HALF_LAT = 3
HALF_LON = 6
RA = 12
WIN = 144
COLS = 48
WINDOWS = 4
OFFS = 2 * WIN_LON - 1
SPAN = OFFS * RA
LINE = WIN_LAT * OFFS
POSITIONS = 4 * WIN_LAT * LINE
SCALE = DH ** (-0.5)
W_CHUNKS = 54
GAIN_AT = 61
HALO = 8
NORTH_AT, EAST_AT, CORNER_AT, FLAT = 0, 384, 440, 512
B_CHUNKS = 5
VMEM = 24 * 1024 * 1024
LOG2E = 1.0 / math.log(2.0)
UNROLL = True
GROUP = 2
TOK = WINDOWS * WIN

LON = ("y", "zh", "c")
LAT = ("zl", "x")
CHIPS = ("y", "zh", "zl", "x")


def nn(a, b):
    return lax.dot_general(a, b, (((1,), (0,)), ((), ())), preferred_element_type=F32)


def nt(a, b):
    return lax.dot_general(a, b, (((1,), (1,)), ((), ())), preferred_element_type=F32)


def tn(a, b):
    return lax.dot_general(a, b, (((0,), (0,)), ((), ())), preferred_element_type=F32)


def put_rows(dst, start, count, rows):
    rows = rows.astype(F32)
    spare = jnp.zeros((count, 256 - D), F32)
    dst[0, pl.ds(start, count, stride=RA), :] = rows[:, :128]
    dst[1, pl.ds(start, count, stride=RA), :] = jnp.concatenate((rows[:, 128:], spare), axis=1)


def put_pair(xs, ys, start, count, ref, l, r):
    pair = ref[l, r, 2].astype(F32)
    rows = pl.ds(start, count, stride=RA)
    xs[0, rows, :] = ref[l, r, 0].astype(F32)
    ys[0, rows, :] = ref[l, r, 1].astype(F32)
    xs[1, rows, :] = pair
    ys[1, rows, :] = pltpu.roll(pair, 64, 1)


def take_pair(src, flat, at, first, second, count):
    first = pl.ds(first, count, stride=RA)
    second = pl.ds(second, count, stride=RA)
    lane = lax.broadcasted_iota(jnp.int32, (count, 128), 1)
    flat[at : at + count, :] = src[0, first, :]
    flat[at + count : at + 2 * count, :] = src[0, second, :]
    flat[at + 2 * count : at + 3 * count, :] = jnp.where(
        lane < 64, src[1, first, :], pltpu.roll(src[1, second, :], 64, 1)
    )


def open_pair(flat, at, count):
    pair = flat[at + 2 * count : at + 3 * count, :]
    return (
        jnp.concatenate((flat[at : at + count, :], pair[:, :64]), axis=1),
        jnp.concatenate((flat[at + count : at + 2 * count, :], pair[:, 64:]), axis=1),
    )


def get_rows(src, start, count):
    low = src[0, pl.ds(start, count, stride=RA), :]
    high = src[1, pl.ds(start, count, stride=RA), :]
    return jnp.concatenate((low, high[:, : D - 128]), axis=1).astype(BF)


def token_rows(src, start, count):
    return jnp.concatenate((src[0, start : start + count, :], src[1, start : start + count, : D - 128]), axis=1)


def each_window(body):
    if UNROLL:
        for w in range(0, WINDOWS, GROUP):
            body(range(w, w + GROUP))
    else:
        pl.loop(0, WINDOWS)(body)


def norm_stats(values):
    mean = jnp.mean(values, axis=-1, keepdims=True)
    centred = values - mean
    variance = jnp.mean(centred * centred, axis=-1, keepdims=True)
    rstd = lax.rsqrt(variance + 1e-05)
    return centred * rstd, rstd


def gelu_pair(u):
    cdf = 0.5 + 0.5 * lax.erf(u * (0.5**0.5))
    slope = cdf + u * jnp.exp(-0.5 * u * u) * (1.0 / math.sqrt(2.0 * math.pi))
    return u * cdf, slope


def norm_back(d_hat, hat, rstd):
    m1 = jnp.mean(d_hat, axis=-1, keepdims=True)
    m2 = jnp.mean(d_hat * hat, axis=-1, keepdims=True)
    return rstd * (d_hat - m1 - hat * m2)


def pack_kernel(both_ref, pa_ref, pb_ref, pc_ref):
    def pack(out, l, r, row, count):
        x = both_ref[l, row].astype(F32)[:count]
        dy = both_ref[2 + l, row].astype(F32)[:count]
        out[l, r, 0] = x[:, :128].astype(BF)
        out[l, r, 1] = dy[:, :128].astype(BF)
        out[l, r, 2] = jnp.concatenate((x[:, 128:], dy[:, 128:]), axis=1).astype(BF)

    for l in range(2):
        for r in range(HALF_LAT):
            pack(pa_ref, l, r, r, COLS)
            pack(pb_ref, l, r, r + HALF_LAT, HALF_LON)
            pack(pc_ref, l, r, r, HALF_LON)


def diagonal_order():
    row = lax.broadcasted_iota(jnp.int32, (SPAN, SPAN), 0)
    col = lax.broadcasted_iota(jnp.int32, (SPAN, SPAN), 1)
    step = lax.shift_right_logical(col * 5462, 16)
    return jnp.where(row == (col - step * RA) * OFFS + OFFS - 1 - step, 1.0, 0.0).astype(BF)


def prepare_kernel(table_ref, w_ref, bias_ref, wqkvt_ref, table, lines, rows_first):
    last = lax.axis_index(LAT) == lax.axis_size(LAT) - 1
    wqkvt_ref[...] = w_ref[:, : 3 * D].T
    for h in range(HEADS):
        lines[h : h + 1, :] = table_ref[h]
    table[...] = jnp.zeros_like(table)
    for li in range(2):
        for ai in range(WIN_LAT):
            place = li * WIN_LAT + ai
            parts = []
            for lj in range(2):
                off = ((li * 2 + lj) * WIN_LAT + ai) * LINE
                parts.append(lines[:, off : off + LINE])
            parts.append(jnp.zeros((8, 384 - SPAN), F32))
            both = jnp.concatenate(parts, axis=1)
            for b in range(3):
                table[b, place * 8 : place * 8 + 8, :] = both[:, 128 * b : 128 * (b + 1)]
    t2 = jnp.concatenate((table[0], table[1], table[2, :, : SPAN - 256]), axis=1)
    hi = t2.astype(BF)
    rest = t2 - hi.astype(F32)
    mid = rest.astype(BF)
    low = (rest - mid.astype(F32)).astype(BF)
    perm = diagonal_order()
    wide = (nn(hi, perm) + nn(mid, perm) + nn(low, perm)) * LOG2E
    wide = jnp.concatenate((wide, jnp.zeros((8 * RA, 384 - SPAN), F32)), axis=1)
    for b in range(3):
        table[b] = wide[:, 128 * b : 128 * (b + 1)]
    key_late = lax.rem(lax.broadcasted_iota(jnp.int32, (WIN, WIN), 0), WIN_LAT) >= HALF_LAT
    query_late = lax.rem(lax.broadcasted_iota(jnp.int32, (WIN, WIN), 1), WIN_LAT) >= HALF_LAT
    split = jnp.logical_and(key_late != query_late, last)
    mask_rows = jnp.where(split, -1e9 * LOG2E, 0.0)
    for h in range(HEADS):
        wide_h = jnp.concatenate([table[b, pl.ds(h, RA, stride=8), :] for b in range(3)], axis=1)
        for oi in range(WIN_LON):
            start = (WIN_LON - 1 - oi) * RA
            rows_first[h, oi * RA : (oi + 1) * RA, :] = wide_h[:, start : start + WIN]
    for h in range(HEADS):
        bias_ref[h] = rows_first[h].T + mask_rows


def block_kernel(
    both_ref, na_ref, nb_ref, nc_ref, w_ref, wqkvt, table_ref, bias,
    mine_ref, send_ref, dp_t, hid, xs,
    ys, probs, heads_t, o_t, do_t, kvs, dss,
    n1s, d_bias, m_acc, g_acc, dw, table,
):
    for l in range(2):
        for r in range(HALF_LAT):
            put_rows(xs, l * 6 + r, COLS, both_ref[l, r + HALF_LAT])
            put_rows(ys, l * 6 + r, COLS, both_ref[2 + l, r + HALF_LAT])
            put_pair(xs, ys, l * 6 + r + HALF_LAT, COLS, na_ref, l, r)
            put_pair(xs, ys, COLS * RA + l * 6 + r, HALF_LON, nb_ref, l, r)
            put_pair(xs, ys, COLS * RA + l * 6 + r + HALF_LAT, HALF_LON, nc_ref, l, r)

    d_bias[...] = jnp.zeros_like(d_bias)
    g_acc[...] = jnp.zeros_like(g_acc)

    g1 = table_ref[HEADS][:, :D]
    g2 = table_ref[HEADS + 1][:, :D]
    w_proj = w_ref[:, 3 * D : 4 * D]
    first = HALF_LON * RA

    hat1, rstd1 = norm_stats(token_rows(xs, first, TOK))
    n1 = (hat1 * g1).astype(BF)
    n1s[...] = n1
    kvs[...] = nn(n1, w_ref[:, D : 3 * D]).astype(BF)

    def attend(ws):
        jobs = [(w, h) for w in ws for h in range(HEADS)]
        rows = {w: pl.ds(w * WIN, WIN) for w in ws}
        parts = [slice(h * DH, (h + 1) * DH) for h in range(HEADS)]
        scores = [
            nn(kvs[rows[w], parts[h]], heads_t[w, parts[h], :]) * (SCALE * LOG2E) + bias[h] for w, h in jobs
        ]
        tops = [jnp.max(s, axis=0, keepdims=True) for s in scores]
        powers = [jnp.exp2(s - top) for s, top in zip(scores, tops)]
        shares = [1.0 / jnp.sum(e, axis=0, keepdims=True) for e in powers]
        for k, (w, h) in enumerate(jobs):
            probs[w, h] = (powers[k] * shares[k]).astype(BF)
        for w, h in jobs:
            o_t[w, parts[h], :] = nn(heads_t[w, 2 * D + h * DH : 2 * D + (h + 1) * DH, :], probs[w, h]).astype(BF)

    for w in range(WINDOWS):
        heads_t[w] = nt(wqkvt[...], n1[w * WIN : (w + 1) * WIN]).astype(BF)
    each_window(attend)
    for w in range(WINDOWS):
        hid[w * WIN : (w + 1) * WIN, :] = tn(o_t[w], w_proj)

    hidden = token_rows(xs, first, TOK) + hid[...]
    hat2, rstd2 = norm_stats(hidden)
    n2 = (hat2 * g2).astype(BF)
    n2_t = n2.T
    dy = token_rows(ys, first, TOK)
    dyb = dy.astype(BF)
    dy_t = dyb.T
    d_n2 = jnp.zeros((TOK, D), F32)
    for j in range(3):
        cols = slice(j * 256, (j + 1) * 256)
        act, slope = gelu_pair(nn(n2, w_ref[:, 4 * D + j * 256 : 4 * D + (j + 1) * 256]))
        d_act = nn(dyb, w_ref[:, 4 * D + MLP + j * 256 : 4 * D + MLP + (j + 1) * 256]).astype(BF).astype(F32)
        d_u = (d_act * slope).astype(BF)
        m_acc[2 * D :, cols] = nn(dy_t, act.astype(BF)).astype(BF)
        m_acc[D : 2 * D, cols] = nn(n2_t, d_u).astype(BF)
        d_n2 = d_n2 + nt(d_u, w_ref[:, 4 * D + j * 256 : 4 * D + (j + 1) * 256])
    d_n2 = d_n2.astype(BF).astype(F32)
    g_acc[1:2, :D] = jnp.sum(d_n2 * hat2, axis=0, keepdims=True)
    d_hidden = dy + norm_back(d_n2 * g2, hat2, rstd2)
    dhb = d_hidden.astype(BF)
    hid[...] = d_hidden
    d_proj = jnp.zeros((D, D), F32)
    for w in range(WINDOWS):
        rows = slice(w * WIN, (w + 1) * WIN)
        d_proj = d_proj + nn(o_t[w], dhb[rows])
        do_t[w] = nt(w_proj, dhb[rows]).astype(BF)

    def attend_back(ws):
        jobs = [(w, h) for w in ws for h in range(HEADS)]
        rows = {w: pl.ds(w * WIN, WIN) for w in ws}
        parts = [slice(h * DH, (h + 1) * DH) for h in range(HEADS)]
        d_probs = [
            nn(kvs[rows[w], D + h * DH : D + (h + 1) * DH], do_t[w, parts[h], :]) for w, h in jobs
        ]
        for k, (w, h) in enumerate(jobs):
            pf = probs[w, h].astype(F32)
            prod = pf * d_probs[k]
            ds = prod - pf * jnp.sum(prod, axis=0, keepdims=True)
            d_bias[h] = d_bias[h] + ds
            dss[k] = ds.astype(BF)
        for k, (w, h) in enumerate(jobs):
            part = parts[h]
            q_t = heads_t[w, part, :]
            k_t = heads_t[w, D + h * DH : D + (h + 1) * DH, :]
            dp_t[w, part, :] = (nn(k_t, dss[k]) * SCALE).astype(BF)
            dp_t[w, D + h * DH : D + (h + 1) * DH, :] = (nt(q_t, dss[k]) * SCALE).astype(BF)
            dp_t[w, 2 * D + h * DH : 2 * D + (h + 1) * DH, :] = nt(do_t[w, part, :], probs[w, h]).astype(BF)

    each_window(attend_back)

    core = lax.axis_index("c")
    perm = diagonal_order()
    dw[...] = jnp.zeros_like(dw)
    d_qkv = jnp.zeros((3 * D, D), F32)
    for w in range(WINDOWS):
        d_qkv = d_qkv + nn(dp_t[w], n1s[w * WIN : (w + 1) * WIN, :])
    m_acc[:D, :] = jnp.concatenate((d_qkv.T, d_proj), axis=1).astype(BF)

    for h in range(HEADS):
        d_bias[h] = d_bias[h].T
    for oi in range(WIN_LON):
        start = (WIN_LON - 1 - oi) * RA
        for h in range(HEADS):
            dw[h * RA : (h + 1) * RA, start : start + WIN] += d_bias[h, oi * RA : (oi + 1) * RA, :]
    dwv = dw[:, :SPAN]
    dw_hi = dwv.astype(BF)
    dw_lo = (dwv - dw_hi.astype(F32)).astype(BF)
    d_t2 = nt(dw_hi, perm) + nt(dw_lo, perm)
    d_t2 = jnp.concatenate((d_t2, jnp.zeros((HEADS * RA, 384 - SPAN), F32)), axis=1)
    table[...] = jnp.zeros_like(table)
    for h in range(HEADS):
        for b in range(3):
            table[b, pl.ds(h, RA, stride=8), :] = d_t2[h * RA : (h + 1) * RA, 128 * b : 128 * (b + 1)]

    mine_half = pl.multiple_of(core * 288, 32)
    send_half = pl.multiple_of((1 - core) * 288, 32)
    for i in range(9):
        for b in range(6):
            cols = slice(b * 128, (b + 1) * 128)
            mine_ref[i * 6 + b] = m_acc[pl.ds(mine_half + 32 * i, 32), cols]
            send_ref[i * 6 + b] = m_acc[pl.ds(send_half + 32 * i, 32), cols]
    zero = jnp.zeros((32, 128), BF)
    for ref, half in ((mine_ref, core), (send_ref, 1 - core)):
        for k in range(W_CHUNKS, 64):
            ref[k] = zero

        @pl.when(half == 0)
        def _(ref=ref):
            for k in range(5):
                ref[W_CHUNKS + k] = table[k % 3, 32 * (k // 3) : 32 * (k // 3) + 32, :].astype(BF)
            ref[W_CHUNKS + B_CHUNKS] = g_acc[:, :128].astype(BF)
            ref[W_CHUNKS + B_CHUNKS + 1] = g_acc[:, 128:].astype(BF)

        @pl.when(half == 1)
        def _(ref=ref):
            for k in range(5, 9):
                ref[W_CHUNKS + k - 5] = table[k % 3, 32 * (k // 3) : 32 * (k // 3) + 32, :].astype(BF)


def grad_kernel(dp_t, hid, xs, w_ref, table_ref, own_ref, halo_ref, gain_ref, gs, flat):
    g1 = table_ref[HEADS][:, :D]
    first = HALF_LON * RA
    gs[:, :first, :] = jnp.zeros((2, first, 128), F32)
    d_n1 = []
    for w in range(WINDOWS):
        d_n1.append(nn(w_ref[:, : 3 * D], dp_t[w]).T)
    d_n1 = jnp.concatenate(d_n1, axis=0).astype(BF).astype(F32)
    hat1, rstd1 = norm_stats(token_rows(xs, first, TOK))
    d_gain = jnp.sum(d_n1 * hat1, axis=0, keepdims=True)
    spare = jnp.zeros((1, 256 - D), F32)
    gain_ref[...] = jnp.concatenate(
        (d_gain[:, :128], jnp.concatenate((d_gain[:, 128:], spare), axis=1), jnp.zeros((30, 128), F32)), axis=0
    ).astype(BF)
    d_x = hid[...] + norm_back(d_n1 * g1, hat1, rstd1)
    gs[0, first:, :] = d_x[:, :128]
    gs[1, first:, : D - 128] = d_x[:, 128:]

    for l in range(2):
        for r in range(HALF_LAT):
            own_ref[l, r] = get_rows(gs, l * 6 + r, COLS)

    flat[...] = jnp.zeros_like(flat)
    inner = COLS - HALF_LON
    for r in range(HALF_LAT):
        late = r + HALF_LAT
        take_pair(gs, flat, NORTH_AT + r * 3 * inner, first + late, first + 6 + late, inner)
        take_pair(gs, flat, EAST_AT + r * 3 * HALF_LON, COLS * RA + r, COLS * RA + r + 6, HALF_LON)
        take_pair(gs, flat, CORNER_AT + r * 3 * HALF_LON, COLS * RA + late, COLS * RA + late + 6, HALF_LON)
    for k in range(64):
        halo_ref[k] = flat[HALO * k : HALO * (k + 1), :].astype(BF)


def join_kernel(mine_ref, got_ref, halo_ref, gain_ref, out_ref):
    for k in range(64):
        if k != GAIN_AT:
            out_ref[k, :32] = (mine_ref[k].astype(F32) + got_ref[k].astype(F32)).astype(BF)
        out_ref[k, 32:] = halo_ref[k]
    out_ref[GAIN_AT, :32] = gain_ref[...]


def reply_kernel(got_ref, out_ref):
    relay = lax.axis_index(CHIPS)
    is_bias = jnp.logical_and(relay >= W_CHUNKS, relay < W_CHUNKS + B_CHUNKS).astype(F32)
    total = jnp.zeros((32, 128), F32)
    bands = []
    for lat in range(8):
        s = got_ref[lat, :32].astype(F32)
        for j in range(1, 8):
            s = s + got_ref[j * 8 + lat, :32].astype(F32)
        bands.append(s)
        total = total + s
    by_lat = jnp.logical_or(relay < EAST_AT // HALO, relay >= CORNER_AT // HALO).astype(jnp.int32)
    by_lon = jnp.logical_and(relay >= EAST_AT // HALO, lax.axis_index("c") == 1).astype(jnp.int32)
    for lat in range(8):
        s = jnp.where(is_bias > 0.5, bands[lat], total).astype(BF)
        from_lat = lax.rem(lat + 7 * by_lat, 8)
        for j in range(8):
            out_ref[j * 8 + lat, :32] = s
            out_ref[j * 8 + lat, 32:] = got_ref[lax.rem(j + 7 * by_lon, 8) * 8 + from_lat, 32:]


def finish_kernel(
    a_ref, b_ref, own_ref,
    dx_ref, dg1_ref, dqkv_ref, dproj_ref, dg2_ref, dup_ref, ddown_ref, dt_ref,
    m_acc, table, g_acc, line, lines, flat, grad_scale,
):
    core = lax.axis_index("c")
    a_half = pl.multiple_of(core * 288, 32)
    b_half = pl.multiple_of((1 - core) * 288, 32)
    for i in range(9):
        for b in range(6):
            cols = slice(b * 128, (b + 1) * 128)
            m_acc[pl.ds(a_half + 32 * i, 32), cols] = a_ref[i * 6 + b, :32].astype(F32) * grad_scale
            m_acc[pl.ds(b_half + 32 * i, 32), cols] = b_ref[i * 6 + b, :32].astype(F32) * grad_scale
    for ref, half in ((a_ref, core), (b_ref, 1 - core)):

        @pl.when(half == 0)
        def _(ref=ref):
            for k in range(5):
                table[k % 3, 32 * (k // 3) : 32 * (k // 3) + 32, :] = ref[W_CHUNKS + k, :32].astype(F32)
            g_acc[:, :128] = ref[W_CHUNKS + B_CHUNKS, :32].astype(F32) * grad_scale
            g_acc[:, 128:] = ref[W_CHUNKS + B_CHUNKS + 1, :32].astype(F32) * grad_scale

        @pl.when(half == 1)
        def _(ref=ref):
            for k in range(5, 9):
                table[k % 3, 32 * (k // 3) : 32 * (k // 3) + 32, :] = ref[W_CHUNKS + k - 5, :32].astype(F32)

    dqkv_ref[...] = m_acc[:D, : 3 * D]
    dproj_ref[...] = m_acc[:D, 3 * D :]
    dup_ref[...] = m_acc[D : 2 * D, :]
    ddown_ref[...] = m_acc[2 * D :, :]
    d_gain = (a_ref[GAIN_AT, :32].astype(F32) + b_ref[GAIN_AT, :32].astype(F32)) * grad_scale
    dg1_ref[:, :128] = d_gain[0:1, :]
    dg1_ref[:, 128:] = d_gain[1:2, : D - 128]
    dg2_ref[...] = g_acc[1:2, :D]
    for li in range(2):
        for ai in range(WIN_LAT):
            place = li * WIN_LAT + ai
            rows = jnp.concatenate([table[b, place * 8 : place * 8 + 8, :] for b in range(3)], axis=1)
            for lj in range(2):
                off = ((li * 2 + lj) * WIN_LAT + ai) * LINE
                lines[:, off : off + LINE] = rows[:, lj * LINE : (lj + 1) * LINE]
    for h in range(HEADS):
        dt_ref[h] = lines[h : h + 1, :]

    for k in range(64):
        ref = a_ref if k < EAST_AT // HALO else b_ref
        flat[HALO * k : HALO * (k + 1), :] = ref[k, 32:].astype(F32)
    inner = COLS - HALF_LON
    for r in range(HALF_LAT):
        north = open_pair(flat, NORTH_AT + r * 3 * inner, inner)
        east = open_pair(flat, EAST_AT + r * 3 * HALF_LON, HALF_LON)
        corner = open_pair(flat, CORNER_AT + r * 3 * HALF_LON, HALF_LON)
        for l in range(2):
            line[...] = own_ref[l, r].astype(F32)
            line[:HALF_LON, :] = east[l]
            dx_ref[l, r + HALF_LAT] = line[...].astype(BF)
            line[HALF_LON:, :] = north[l]
            line[:HALF_LON, :] = corner[l]
            dx_ref[l, r] = line[...].astype(BF)


def shift_pairs(lon_by, lat_by):
    pairs = []
    for lon in range(16):
        for lat in range(8):
            pairs.append((lon * 8 + lat, ((lon + lon_by) % 16) * 8 + (lat + lat_by) % 8))
    return pairs


def one_axis(length, by):
    return [(i, (i + by) % length) for i in range(length)]


def vmem_spec():
    return pl.BlockSpec(memory_space=pltpu.VMEM)


def prepare(table, weights):
    shape = jax.ShapeDtypeStruct
    return pl.pallas_call(
        prepare_kernel,
        out_shape=(shape((HEADS, WIN, WIN), F32), shape((3 * D, D), BF)),
        in_specs=[vmem_spec()] * 2,
        out_specs=[vmem_spec()] * 2,
        scratch_shapes=[
            pltpu.VMEM((3, 8 * RA, 128), F32),
            pltpu.VMEM((8, POSITIONS), F32),
            pltpu.VMEM((HEADS, WIN, WIN), F32),
        ],
        compiler_params=pltpu.CompilerParams(vmem_limit_bytes=VMEM),
    )(table, weights)


def pack_halos(both):
    shape = jax.ShapeDtypeStruct
    return pl.pallas_call(
        pack_kernel,
        out_shape=(
            shape((2, HALF_LAT, 3, COLS, 128), BF),
            shape((2, HALF_LAT, 3, HALF_LON, 128), BF),
            shape((2, HALF_LAT, 3, HALF_LON, 128), BF),
        ),
        in_specs=[vmem_spec()],
        out_specs=[vmem_spec()] * 3,
        compiler_params=pltpu.CompilerParams(vmem_limit_bytes=VMEM),
    )(both)


def run_block(both, na, nb, nc, weights, w_qkv_t, table, bias):
    shape = jax.ShapeDtypeStruct
    return pl.pallas_call(
        block_kernel,
        out_shape=(
            shape((64, 32, 128), BF),
            shape((64, 32, 128), BF),
            shape((WINDOWS, 3 * D, WIN), BF),
            shape((TOK, D), F32),
            shape((2, 54 * RA, 128), F32),
        ),
        in_specs=[vmem_spec()] * 8,
        out_specs=[vmem_spec()] * 5,
        scratch_shapes=[
            pltpu.VMEM((2, 54 * RA, 128), F32),
            pltpu.VMEM((WINDOWS, HEADS, WIN, WIN), BF),
            pltpu.VMEM((WINDOWS, 3 * D, WIN), BF),
            pltpu.VMEM((WINDOWS, D, WIN), BF),
            pltpu.VMEM((WINDOWS, D, WIN), BF),
            pltpu.VMEM((TOK, 2 * D), BF),
            pltpu.VMEM((WINDOWS * HEADS, WIN, WIN), BF),
            pltpu.VMEM((TOK, D), BF),
            pltpu.VMEM((HEADS, WIN, WIN), F32),
            pltpu.VMEM((3 * D, MLP), BF),
            pltpu.VMEM((32, 256), F32),
            pltpu.VMEM((HEADS * RA, 384), F32),
            pltpu.VMEM((3, 8 * RA, 128), F32),
        ],
        compiler_params=pltpu.CompilerParams(vmem_limit_bytes=VMEM),
    )(both, na, nb, nc, weights, w_qkv_t, table, bias)


def input_grad(d_packed_t, d_hidden, tokens, weights, table):
    shape = jax.ShapeDtypeStruct
    return pl.pallas_call(
        grad_kernel,
        out_shape=(
            shape((2, HALF_LAT, COLS, D), BF),
            shape((64, HALO, 128), BF),
            shape((32, 128), BF),
        ),
        in_specs=[vmem_spec()] * 5,
        out_specs=[vmem_spec()] * 3,
        scratch_shapes=[pltpu.VMEM((2, 54 * RA, 128), F32), pltpu.VMEM((FLAT, 128), F32)],
        compiler_params=pltpu.CompilerParams(vmem_limit_bytes=VMEM),
    )(d_packed_t, d_hidden, tokens, weights, table)


def local(tokens, cotangent, ln1_gain, w_qkv, w_proj, ln2_gain, w_up, w_down, bias_table):
    edge = ((0, 0),) * 3
    both = jnp.pad(tokens, ((0, 2),) + edge) + jnp.pad(cotangent, ((2, 0),) + edge)
    part_a, part_b, part_c = pack_halos(both)
    na = lax.ppermute(part_a, LAT, one_axis(8, -1))
    nb = lax.ppermute(part_b, LON, one_axis(16, -1))
    nc = lax.ppermute(part_c, LON + LAT, shift_pairs(-1, -1))

    weights = jnp.concatenate((w_qkv, w_proj, w_up, w_down.T), axis=1)
    gains = jnp.pad(jnp.stack((ln1_gain, ln2_gain)), ((0, 0), (0, POSITIONS - D)))
    table = jnp.concatenate((bias_table.reshape(HEADS, 1, POSITIONS), gains[:, None]), axis=0)
    bias, w_qkv_t = prepare(table, weights)
    mine, send, d_packed_t, d_hidden, shifted = run_block(both, na, nb, nc, weights, w_qkv_t, table, bias)

    pair = [(0, 1), (1, 0)]
    got = lax.ppermute(send, "c", pair)
    own, halo, gain = input_grad(d_packed_t, d_hidden, shifted, weights, table)
    chunks = jax.ShapeDtypeStruct((64, 32 + HALO, 128), BF)
    joined = pl.pallas_call(
        join_kernel,
        out_shape=chunks,
        in_specs=[vmem_spec()] * 4,
        out_specs=vmem_spec(),
        compiler_params=pltpu.CompilerParams(vmem_limit_bytes=VMEM),
    )(mine, got, halo, gain)
    spread = lax.all_to_all(joined, CHIPS, 0, 0, tiled=True)
    reply = pl.pallas_call(
        reply_kernel,
        out_shape=chunks,
        in_specs=[vmem_spec()],
        out_specs=vmem_spec(),
        compiler_params=pltpu.CompilerParams(vmem_limit_bytes=VMEM),
    )(spread)
    half_a = lax.all_to_all(reply, CHIPS, 0, 0, tiled=True)
    half_b = lax.ppermute(half_a, "c", pair)
    shape = jax.ShapeDtypeStruct
    total_tokens = 128 * tokens.shape[0] * tokens.shape[1] * tokens.shape[2]
    dx, dg1, dqkv, dproj, dg2, dup, ddown, dt = pl.pallas_call(
        functools.partial(finish_kernel, grad_scale=1.0 / math.sqrt(total_tokens)),
        out_shape=(
            shape(tokens.shape, BF),
            shape((1, D), F32),
            shape((D, 3 * D), F32),
            shape((D, D), F32),
            shape((1, D), F32),
            shape((D, MLP), F32),
            shape((D, MLP), F32),
            shape((HEADS, 1, POSITIONS), F32),
        ),
        in_specs=[vmem_spec()] * 3,
        out_specs=[vmem_spec()] * 8,
        scratch_shapes=[
            pltpu.VMEM((3 * D, MLP), F32),
            pltpu.VMEM((3, 8 * RA, 128), F32),
            pltpu.VMEM((32, 256), F32),
            pltpu.VMEM((COLS, D), F32),
            pltpu.VMEM((8, POSITIONS), F32),
            pltpu.VMEM((FLAT, 128), F32),
        ],
        compiler_params=pltpu.CompilerParams(vmem_limit_bytes=VMEM),
    )(half_a, half_b, own)
    return (
        dx,
        dg1.reshape(D),
        dqkv,
        dproj,
        dg2.reshape(D),
        dup,
        ddown.T,
        dt.reshape(1, HEADS, POSITIONS),
    )


def solution(mesh):
    parts = Mesh(mesh.devices.reshape(4, 2, 2, 2, 4), ("y", "zh", "c", "zl", "x"))
    grid = P(None, LAT, LON, None)
    in_specs = (grid, grid, P(), P(), P(), P(), P(), P(), P(LAT, None, None))
    out_specs = (grid, P(), P(), P(), P(), P(), P(), P(LAT, None, None))
    return jax.shard_map(local, mesh=parts, in_specs=in_specs, out_specs=out_specs, check_vma=False)
```

profile of v0, /device:TPU:1, one launch (start us, length us, event | category | flops | bytes accessed | tf_op | source)
XLA Modules:
  0.0 72.9 jit_solution(15573176438711292220)
XLA Ops:
  0.6 0.0 copy-start.5
  0.6 0.0 copy-start.6
  0.7 0.0 copy-start.4
  0.7 0.0 copy-start.1
  0.7 0.0 copy-start
  0.7 1.2 %pad_add_fusion.both_ref = bf16[4,6,48,192]{3,2,1,0:T(8,128)(2,1)S(1)} fusion(bf16[2,6,48,192]{3,2,1,0:T(8,128)(2,1)} %param.10, bf16[2,6,48,192]{3,2,1,0:T(8,128)(2,1)} %param.9), kind=kLoop, calls=%fused_computation | loop fusion | flops 221184 | bytes 884736 | tf_op jit(solution)/shard_map/add | solution.py:562
  1.9 0.1 shard_map.152
  2.0 1.5 %collective-permute-start.1 = (bf16[2,3,3,6,128]{4,3,2,1,0:T(8,128)(2,1)S(1)}, bf16[2,3,3,6,128]{4,3,2,1,0:T(8,128)(2,1)S(1)}, u32[]{:S(2)}, u32[]{:S(2)}) collective-permute-start(bf16[2,3,3,6,128]{4,3,2,1,0:T(8,128)(2,1)S(1)} %get-tuple-element.30), channel_id=1, source_target_pairs={{0,120},{8,0},{16,8},{24,16},{32,24},{40,32},{48,40},{56,48},{64,5... | collective-permute-start | bytes 82952 | tf_op jit(solution)/shard_map/ppermute | solution.py:565
  3.5 8.7 %collective-permute-start.2 = (bf16[2,3,3,6,128]{4,3,2,1,0:T(8,128)(2,1)S(1)}, bf16[2,3,3,6,128]{4,3,2,1,0:T(8,128)(2,1)S(1)}, u32[]{:S(2)}, u32[]{:S(2)}) collective-permute-start(bf16[2,3,3,6,128]{4,3,2,1,0:T(8,128)(2,1)S(1)} %get-tuple-element.31), channel_id=1, source_target_pairs={{0,127},{1,120},{2,121},{3,122},{4,123},{5,124},{6,125},{7,126},{8... | collective-permute-start | bytes 82952 | tf_op jit(solution)/shard_map/ppermute | solution.py:566
  12.2 0.5 collective-permute-start
  12.8 0.0 copy-done.4
  12.8 0.1 pad_maximum_fusion.table_ref
  12.9 0.0 copy-done.1
  12.9 0.0 copy-done
  12.9 0.0 copy-done.3
  12.9 0.0 copy-done.2
  13.0 0.3 concatenate.6.w_ref
  13.3 1.2 %shard_map.153 = (f32[6,144,144]{2,1,0:T(8,128)S(1)}, bf16[576,192]{1,0:T(8,128)(2,1)S(1)}) custom-call(f32[8,1,3312]{2,1,0:T(1,128)S(1)} %pad_maximum_fusion.table_ref, bf16[192,2304]{1,0:T(8,128)(2,1)S(1)} %concatenate.6.w_ref), custom_call_target="tpu_custom_call" | custom-call | tf_op jit(solution)/shard_map/pallas_call | solution.py:483
  14.5 0.0 collective-permute-done.1.nb_ref
  14.5 0.0 collective-permute-done.2.nc_ref
  14.5 4.5 %collective-permute-done.na_ref = bf16[2,3,3,48,128]{4,3,2,1,0:T(8,128)(2,1)S(1)} collective-permute-done((bf16[2,3,3,48,128]{4,3,2,1,0:T(8,128)(2,1)S(1)}, bf16[2,3,3,48,128]{4,3,2,1,0:T(8,128)(2,1)S(1)}, u32[]{:S(2)}, u32[]{:S(2)}) %collective-permute-start) | collective-permute-done | bytes 221216 | tf_op jit(solution)/shard_map/ppermute | solution.py:564
  19.0 8.5 %shard_map.154 = (bf16[64,32,128]{2,1,0:T(8,128)(2,1)S(1)}, bf16[64,32,128]{2,1,0:T(8,128)(2,1)S(1)}, bf16[4,576,144]{2,1,0:T(8,128)(2,1)S(1)}, f32[576,192]{1,0:T(8,128)S(1)}, f32[2,648,128]{2,1,0:T(8,128)S(1)}) custom-call(bf16[4,6,48,192]{3,2,1,0:T(8,128)(2,1)S(1)} %pad_add_fusion.both_ref, bf16[2,3,3,48,128]{4,3,2,1,0:T(8,128)(2,1)S(1)} %collective-permute-done.na_ref, ...), custom_call_target="tpu_custom_call" | custom-call | tf_op jit(solution)/shard_map/pallas_call | solution.py:514
  27.5 1.1 %collective-permute-start.3 = (bf16[64,32,128]{2,1,0:T(8,128)(2,1)S(1)}, bf16[64,32,128]{2,1,0:T(8,128)(2,1)S(1)}, u32[]{:S(2)}, u32[]{:S(2)}) collective-permute-start(bf16[64,32,128]{2,1,0:T(8,128)(2,1)S(1)} %get-tuple-element.35), channel_id=1, source_target_pairs={{0,8},{8,0},{1,9},{9,1},{2,10},{10,2},{3,11},{11,3},{4,12},{12,4},... | collective-permute-start | bytes 1572872 | tf_op jit(solution)/shard_map/ppermute | solution.py:575
  28.6 0.9 %shard_map.155 = (bf16[2,3,48,192]{3,2,1,0:T(8,128)(2,1)S(1)}, bf16[64,8,128]{2,1,0:T(8,128)(2,1)S(1)}, bf16[32,128]{1,0:T(8,128)(2,1)S(1)}) custom-call(bf16[4,576,144]{2,1,0:T(8,128)(2,1)S(1)} %get-tuple-element.36.dp_t, f32[576,192]{1,0:T(8,128)S(1)} %get-tuple-element.37.hid, f32[2,648,128]{2,1,0:T(8,128)S(1)} %get-tuple-element.38.xs, ...), custom_call_target="tpu_custom_call" | custom-call | tf_op jit(solution)/shard_map/pallas_call | solution.py:546
  29.6 0.6 collective-permute-done.3.got_ref
  30.2 0.1 shard_map.156
  30.3 19.1 %all_to_all.10.got_ref = bf16[64,40,128]{2,1,0:T(8,128)(2,1)S(1)} all-to-all(bf16[64,40,128]{2,1,0:T(8,128)(2,1)S(1)} %shard_map.156), channel_id=1, replica_groups=mesh['y'=4,'zh'=2,'c'=2,'zl'=2,'x'=4] {'y','zh','zl','x'}, dimensions={0} | all-to-all | bytes 1310720 | tf_op jit(solution)/shard_map/all_to_all | solution.py:585
  49.4 0.1 shard_map.157
  49.5 16.9 %all_to_all.11.a_ref = bf16[64,40,128]{2,1,0:T(8,128)(2,1)S(1)} all-to-all(bf16[64,40,128]{2,1,0:T(8,128)(2,1)S(1)} %shard_map.157), channel_id=1, replica_groups=mesh['y'=4,'zh'=2,'c'=2,'zl'=2,'x'=4] {'y','zh','zl','x'}, dimensions={0} | all-to-all | bytes 1310720 | tf_op jit(solution)/shard_map/all_to_all | solution.py:593
  66.4 3.1 %collective-permute-start.4 = (bf16[64,40,128]{2,1,0:T(8,128)(2,1)S(1)}, bf16[64,40,128]{2,1,0:T(8,128)(2,1)S(1)}, u32[]{:S(2)}, u32[]{:S(2)}) collective-permute-start(bf16[64,40,128]{2,1,0:T(8,128)(2,1)S(1)} %all_to_all.11.a_ref), channel_id=1, source_target_pairs={{0,8},{8,0},{1,9},{9,1},{2,10},{10,2},{3,11},{11,3},{4,12},{12,4},... | collective-permute-start | bytes 1966088 | tf_op jit(solution)/shard_map/ppermute | solution.py:594
  69.5 1.7 %collective-permute-done.4.b_ref = bf16[64,40,128]{2,1,0:T(8,128)(2,1)S(1)} collective-permute-done((bf16[64,40,128]{2,1,0:T(8,128)(2,1)S(1)}, bf16[64,40,128]{2,1,0:T(8,128)(2,1)S(1)}, u32[]{:S(2)}, u32[]{:S(2)}) %collective-permute-start.4) | collective-permute-done | bytes 655392 | tf_op jit(solution)/shard_map/ppermute | solution.py:594
  71.2 1.7 %shard_map.158 = (bf16[2,6,48,192]{3,2,1,0:T(8,128)(2,1)}, f32[1,192]{1,0:T(1,128)}, f32[192,576]{1,0:T(8,128)}, f32[192,192]{1,0:T(8,128)}, f32[1,192]{1,0:T(1,...) custom-call(bf16[64,40,128]{2,1,0:T(8,128)(2,1)S(1)} %all_to_all.11.a_ref, ...), custom_call_target="tpu_custom_call" | custom-call | tf_op jit(solution)/shard_map/pallas_call | solution.py:597
  (6 shorter events, 0.0 us)
Async XLA Ops:
  0.6 12.1 %copy-start.5 = (f32[192]{0:T(256)S(1)}, f32[192]{0:T(256)}, u32[]{:S(2)}) copy-start(f32[192]{0:T(256)} %param.14) | copy-start | bytes 2308
  0.6 12.1 %copy-start.6 = (f32[192]{0:T(256)S(1)}, f32[192]{0:T(256)}, u32[]{:S(2)}) copy-start(f32[192]{0:T(256)} %param.11) | copy-start | bytes 2308
  0.7 12.1 %copy-start.4 = (f32[1,6,3312]{2,0,1:T(1,128)S(1)}, f32[1,6,3312]{2,0,1:T(1,128)}, u32[]{:S(2)}) copy-start(f32[1,6,3312]{2,0,1:T(1,128)} %param.17) | copy-start | bytes 238468
  0.7 12.2 %copy-start.1 = (bf16[768,192]{0,1:T(8,128)(2,1)S(1)}, bf16[768,192]{0,1:T(8,128)(2,1)}, u32[]{:S(2)}) copy-start(bf16[768,192]{0,1:T(8,128)(2,1)} %param.16) | copy-start | bytes 884740
  0.7 12.2 %copy-start = (bf16[192,768]{1,0:T(8,128)(2,1)S(1)}, bf16[192,768]{1,0:T(8,128)(2,1)}, u32[]{:S(2)}) copy-start(bf16[192,768]{1,0:T(8,128)(2,1)} %param.15) | copy-start | bytes 884740
  0.7 12.2 %copy-start.3 = (bf16[192,192]{1,0:T(8,128)(2,1)S(1)}, bf16[192,192]{1,0:T(8,128)(2,1)}, u32[]{:S(2)}) copy-start(bf16[192,192]{1,0:T(8,128)(2,1)} %param.13) | copy-start | bytes 221188
  0.7 12.2 %copy-start.2 = (bf16[192,576]{1,0:T(8,128)(2,1)S(1)}, bf16[192,576]{1,0:T(8,128)(2,1)}, u32[]{:S(2)}) copy-start(bf16[192,576]{1,0:T(8,128)(2,1)} %param.12) | copy-start | bytes 663556
  2.0 12.4 %collective-permute-start.1 = (bf16[2,3,3,6,128]{4,3,2,1,0:T(8,128)(2,1)S(1)}, bf16[2,3,3,6,128]{4,3,2,1,0:T(8,128)(2,1)S(1)}, u32[]{:S(2)}, u32[]{:S(2)}) collective-permute-start(bf16[2,3,3,6,128]{4,3,2,1,0:T(8,128)(2,1)S(1)} %get-tuple-element.30), channel_id=1, source_target_pairs={{0,120},{8,0},{16,8},{24,16},{32,24},{40,32},{48,40},{56,48},{64,5... | collective-permute-start | bytes 82952 | tf_op jit(solution)/shard_map/ppermute | solution.py:565
  3.5 10.9 %collective-permute-start.2 = (bf16[2,3,3,6,128]{4,3,2,1,0:T(8,128)(2,1)S(1)}, bf16[2,3,3,6,128]{4,3,2,1,0:T(8,128)(2,1)S(1)}, u32[]{:S(2)}, u32[]{:S(2)}) collective-permute-start(bf16[2,3,3,6,128]{4,3,2,1,0:T(8,128)(2,1)S(1)} %get-tuple-element.31), channel_id=1, source_target_pairs={{0,127},{1,120},{2,121},{3,122},{4,123},{5,124},{6,125},{7,126},{8... | collective-permute-start | bytes 82952 | tf_op jit(solution)/shard_map/ppermute | solution.py:566
  12.2 6.8 %collective-permute-start = (bf16[2,3,3,48,128]{4,3,2,1,0:T(8,128)(2,1)S(1)}, bf16[2,3,3,48,128]{4,3,2,1,0:T(8,128)(2,1)S(1)}, u32[]{:S(2)}, u32[]{:S(2)}) collective-permute-start(bf16[2,3,3,48,128]{4,3,2,1,0:T(8,128)(2,1)S(1)} %get-tuple-element.29), channel_id=1, source_target_pairs={{0,7},{1,0},{2,1},{3,2},{4,3},{5,4},{6,5},{7,6},{8,15},{9,8},{10,9... | collective-permute-start | bytes 663560 | tf_op jit(solution)/shard_map/ppermute | solution.py:564
  27.5 2.6 %collective-permute-start.3 = (bf16[64,32,128]{2,1,0:T(8,128)(2,1)S(1)}, bf16[64,32,128]{2,1,0:T(8,128)(2,1)S(1)}, u32[]{:S(2)}, u32[]{:S(2)}) collective-permute-start(bf16[64,32,128]{2,1,0:T(8,128)(2,1)S(1)} %get-tuple-element.35), channel_id=1, source_target_pairs={{0,8},{8,0},{1,9},{9,1},{2,10},{10,2},{3,11},{11,3},{4,12},{12,4},... | collective-permute-start | bytes 1572872 | tf_op jit(solution)/shard_map/ppermute | solution.py:575
  66.4 4.8 %collective-permute-start.4 = (bf16[64,40,128]{2,1,0:T(8,128)(2,1)S(1)}, bf16[64,40,128]{2,1,0:T(8,128)(2,1)S(1)}, u32[]{:S(2)}, u32[]{:S(2)}) collective-permute-start(bf16[64,40,128]{2,1,0:T(8,128)(2,1)S(1)} %all_to_all.11.a_ref), channel_id=1, source_target_pairs={{0,8},{8,0},{1,9},{9,1},{2,10},{10,2},{3,11},{11,3},{4,12},{12,4},... | collective-permute-start | bytes 1966088 | tf_op jit(solution)/shard_map/ppermute | solution.py:594
where the time goes:
time: 73.1 us; the launch traced here: 72.9 us
  blocking collectives  36 us (49%)
  starting transfers between devices  14.9 us (20%)
  Pallas kernels  12.7 us (17%)
  waiting for transfers between devices  6.86 us (9%)
  other arithmetic  1.34 us (2%)
  between operations  0.81 us (1%)
    all_to_all x1, blocking collectives, local(): spread = lax.all_to_all(joined, CHIPS, 0, 0, tiled=True)  19.1 us
    all_to_all x1, blocking collectives, local(): half_a = lax.all_to_all(reply, CHIPS, 0, 0, tiled=True)  16.9 us
    ppermute x1, starting transfers between devices, local(): nc = lax.ppermute(part_c, LON + LAT, shift_pairs(-1, -1))  8.67 us
    pallas_call x1, Pallas kernels, run_block(): pl.pallas_call(block_kernel, out_shape=(shape((64, 32, 128), BF), shape((...  8.49 us
    ppermute x1, waiting for transfers between devices, local(): na = lax.ppermute(part_a, LAT, one_axis(8, -1))  4.54 us
    ppermute x1, starting transfers between devices, local(): half_b = lax.ppermute(half_a, 'c', pair)  3.07 us
    ppermute x1, waiting for transfers between devices, local(): half_b = lax.ppermute(half_a, 'c', pair)  1.72 us
    pallas_call x1, Pallas kernels, local(): pl.pallas_call(functools.partial(finish_kernel, grad_scale=1.0 / math.sqr...  1.7 us
  transfers between devices with their start and end apart: 5, of which 3 were waited for; matrix products, arithmetic and copies ran while one was open for 1% of the time, Pallas kernels for 3%

commit v1 on v0

--- a/solution.py
+++ b/solution.py
@@ -22,6 +22,7 @@
 RA = 12
 WIN = 144
 COLS = 48
+INNER = COLS - HALF_LON
 WINDOWS = 4
 OFFS = 2 * WIN_LON - 1
 SPAN = OFFS * RA
@@ -63,13 +64,16 @@
     dst[1, pl.ds(start, count, stride=RA), :] = jnp.concatenate((rows[:, 128:], spare), axis=1)
 
 
+def put_parts(xs, ys, start, count, parts):
+    rows = pl.ds(start, count, stride=RA)
+    xs[0, rows, :] = parts[0]
+    ys[0, rows, :] = parts[1]
+    xs[1, rows, :] = parts[2]
+    ys[1, rows, :] = pltpu.roll(parts[2], 64, 1)
+
+
 def put_pair(xs, ys, start, count, ref, l, r):
-    pair = ref[l, r, 2].astype(F32)
-    rows = pl.ds(start, count, stride=RA)
-    xs[0, rows, :] = ref[l, r, 0].astype(F32)
-    ys[0, rows, :] = ref[l, r, 1].astype(F32)
-    xs[1, rows, :] = pair
-    ys[1, rows, :] = pltpu.roll(pair, 64, 1)
+    put_parts(xs, ys, start, count, [ref[l, r, k].astype(F32) for k in range(3)])
 
 
 def take_pair(src, flat, at, first, second, count):
@@ -130,18 +134,19 @@
 
 
 def pack_kernel(both_ref, pa_ref, pb_ref, pc_ref):
-    def pack(out, l, r, row, count):
-        x = both_ref[l, row].astype(F32)[:count]
-        dy = both_ref[2 + l, row].astype(F32)[:count]
-        out[l, r, 0] = x[:, :128].astype(BF)
-        out[l, r, 1] = dy[:, :128].astype(BF)
-        out[l, r, 2] = jnp.concatenate((x[:, 128:], dy[:, 128:]), axis=1).astype(BF)
+    def parts(l, row, cols):
+        x = both_ref[l, row].astype(F32)[cols]
+        dy = both_ref[2 + l, row].astype(F32)[cols]
+        return [x[:, :128], dy[:, :128], jnp.concatenate((x[:, 128:], dy[:, 128:]), axis=1)]
 
     for l in range(2):
         for r in range(HALF_LAT):
-            pack(pa_ref, l, r, r, COLS)
-            pack(pb_ref, l, r, r + HALF_LAT, HALF_LON)
-            pack(pc_ref, l, r, r, HALF_LON)
+            rows = parts(l, r, slice(HALF_LON, COLS)) + [jnp.zeros((128 - 3 * INNER, 128), F32)]
+            pa_ref[l, r] = jnp.concatenate(rows, axis=0).astype(BF)
+            for k, rows in enumerate(parts(l, r + HALF_LAT, slice(0, HALF_LON))):
+                pb_ref[l, r, k] = rows.astype(BF)
+            for k, rows in enumerate(parts(l, r, slice(0, HALF_LON))):
+                pc_ref[l, r, k] = rows.astype(BF)
 
 
 def diagonal_order():
@@ -201,7 +206,9 @@
         for r in range(HALF_LAT):
             put_rows(xs, l * 6 + r, COLS, both_ref[l, r + HALF_LAT])
             put_rows(ys, l * 6 + r, COLS, both_ref[2 + l, r + HALF_LAT])
-            put_pair(xs, ys, l * 6 + r + HALF_LAT, COLS, na_ref, l, r)
+            north = na_ref[l, r].astype(F32)
+            north = [north[k * INNER : (k + 1) * INNER] for k in range(3)]
+            put_parts(xs, ys, HALF_LON * RA + l * 6 + r + HALF_LAT, INNER, north)
             put_pair(xs, ys, COLS * RA + l * 6 + r, HALF_LON, nb_ref, l, r)
             put_pair(xs, ys, COLS * RA + l * 6 + r + HALF_LAT, HALF_LON, nc_ref, l, r)
 
@@ -499,7 +506,7 @@
     return pl.pallas_call(
         pack_kernel,
         out_shape=(
-            shape((2, HALF_LAT, 3, COLS, 128), BF),
+            shape((2, HALF_LAT, 128, 128), BF),
             shape((2, HALF_LAT, 3, HALF_LON, 128), BF),
             shape((2, HALF_LAT, 3, HALF_LON, 128), BF),
         ),

time: 73.1 us -> 72.8 us (level)
  no operation moved by 1% of the time
where the time goes in v1:
time: 72.8 us; the launch traced here: 72.5 us
  blocking collectives  36 us (49%)
  starting transfers between devices  14.9 us (20%)
  Pallas kernels  12.8 us (18%)
  waiting for transfers between devices  6.35 us (9%)
  other arithmetic  1.34 us (2%)
  between operations  0.81 us (1%)
    all_to_all x1, blocking collectives, local(): spread = lax.all_to_all(joined, CHIPS, 0, 0, tiled=True)  19.1 us
    all_to_all x1, blocking collectives, local(): half_a = lax.all_to_all(reply, CHIPS, 0, 0, tiled=True)  16.9 us
    ppermute x1, starting transfers between devices, local(): nc = lax.ppermute(part_c, LON + LAT, shift_pairs(-1, -1))  8.67 us
    pallas_call x1, Pallas kernels, run_block(): pl.pallas_call(block_kernel, out_shape=(shape((64, 32, 128), BF), shape((...  8.63 us
    ppermute x1, waiting for transfers between devices, local(): na = lax.ppermute(part_a, LAT, one_axis(8, -1))  4.01 us
    ppermute x1, starting transfers between devices, local(): half_b = lax.ppermute(half_a, 'c', pair)  3.07 us
    ppermute x1, waiting for transfers between devices, local(): half_b = lax.ppermute(half_a, 'c', pair)  1.72 us
    pallas_call x1, Pallas kernels, local(): pl.pallas_call(functools.partial(finish_kernel, grad_scale=1.0 / math.sqr...  1.7 us
  transfers between devices with their start and end apart: 5, of which 3 were waited for; matrix products, arithmetic and copies ran while one was open for 1% of the time, Pallas kernels for 3%

profile of v1, /device:TPU:1, one launch (start us, length us, event | category | flops | bytes accessed | tf_op | source)
XLA Modules:
  0.0 72.5 jit_solution(15023063885894824008)
XLA Ops:
  0.6 0.0 copy-start.5
  0.6 0.0 copy-start.6
  0.7 0.0 copy-start.4
  0.7 0.0 copy-start.1
  0.7 0.0 copy-start
  0.7 1.2 %pad_add_fusion.both_ref = bf16[4,6,48,192]{3,2,1,0:T(8,128)(2,1)S(1)} fusion(bf16[2,6,48,192]{3,2,1,0:T(8,128)(2,1)} %param.10, bf16[2,6,48,192]{3,2,1,0:T(8,128)(2,1)} %param.9), kind=kLoop, calls=%fused_computation | loop fusion | flops 221184 | bytes 884736 | tf_op jit(solution)/shard_map/add | solution.py:569
  1.9 0.1 shard_map.152
  2.1 1.5 %collective-permute-start.1 = (bf16[2,3,3,6,128]{4,3,2,1,0:T(8,128)(2,1)S(1)}, bf16[2,3,3,6,128]{4,3,2,1,0:T(8,128)(2,1)S(1)}, u32[]{:S(2)}, u32[]{:S(2)}) collective-permute-start(bf16[2,3,3,6,128]{4,3,2,1,0:T(8,128)(2,1)S(1)} %get-tuple-element.30), channel_id=1, source_target_pairs={{0,120},{8,0},{16,8},{24,16},{32,24},{40,32},{48,40},{56,48},{64,5... | collective-permute-start | bytes 82952 | tf_op jit(solution)/shard_map/ppermute | solution.py:572
  3.5 8.7 %collective-permute-start.2 = (bf16[2,3,3,6,128]{4,3,2,1,0:T(8,128)(2,1)S(1)}, bf16[2,3,3,6,128]{4,3,2,1,0:T(8,128)(2,1)S(1)}, u32[]{:S(2)}, u32[]{:S(2)}) collective-permute-start(bf16[2,3,3,6,128]{4,3,2,1,0:T(8,128)(2,1)S(1)} %get-tuple-element.31), channel_id=1, source_target_pairs={{0,127},{1,120},{2,121},{3,122},{4,123},{5,124},{6,125},{7,126},{8... | collective-permute-start | bytes 82952 | tf_op jit(solution)/shard_map/ppermute | solution.py:573
  12.2 0.5 collective-permute-start
  12.8 0.0 copy-done.4
  12.8 0.1 pad_maximum_fusion.table_ref
  12.9 0.0 copy-done.1
  12.9 0.0 copy-done
  12.9 0.0 copy-done.3
  13.0 0.0 copy-done.2
  13.0 0.3 concatenate.6.w_ref
  13.3 1.2 %shard_map.153 = (f32[6,144,144]{2,1,0:T(8,128)S(1)}, bf16[576,192]{1,0:T(8,128)(2,1)S(1)}) custom-call(f32[8,1,3312]{2,1,0:T(1,128)S(1)} %pad_maximum_fusion.table_ref, bf16[192,2304]{1,0:T(8,128)(2,1)S(1)} %concatenate.6.w_ref), custom_call_target="tpu_custom_call" | custom-call | tf_op jit(solution)/shard_map/pallas_call | solution.py:490
  14.5 0.0 collective-permute-done.1.nb_ref
  14.5 0.0 collective-permute-done.2.nc_ref
  14.5 4.0 %collective-permute-done.na_ref = bf16[2,3,128,128]{3,2,1,0:T(8,128)(2,1)S(1)} collective-permute-done((bf16[2,3,128,128]{3,2,1,0:T(8,128)(2,1)S(1)}, bf16[2,3,128,128]{3,2,1,0:T(8,128)(2,1)S(1)}, u32[]{:S(2)}, u32[]{:S(2)}) %collective-permute-start) | collective-permute-done | bytes 196640 | tf_op jit(solution)/shard_map/ppermute | solution.py:571
  18.5 8.6 %shard_map.154 = (bf16[64,32,128]{2,1,0:T(8,128)(2,1)S(1)}, bf16[64,32,128]{2,1,0:T(8,128)(2,1)S(1)}, bf16[4,576,144]{2,1,0:T(8,128)(2,1)S(1)}, f32[576,192]{1,0:T(8,128)S(1)}, f32[2,648,128]{2,1,0:T(8,128)S(1)}) custom-call(bf16[4,6,48,192]{3,2,1,0:T(8,128)(2,1)S(1)} %pad_add_fusion.both_ref, bf16[2,3,128,128]{3,2,1,0:T(8,128)(2,1)S(1)} %collective-permute-done.na_ref, ...), custom_call_target="tpu_custom_call" | custom-call | tf_op jit(solution)/shard_map/pallas_call | solution.py:521
  27.1 1.1 %collective-permute-start.3 = (bf16[64,32,128]{2,1,0:T(8,128)(2,1)S(1)}, bf16[64,32,128]{2,1,0:T(8,128)(2,1)S(1)}, u32[]{:S(2)}, u32[]{:S(2)}) collective-permute-start(bf16[64,32,128]{2,1,0:T(8,128)(2,1)S(1)} %get-tuple-element.35), channel_id=1, source_target_pairs={{0,8},{8,0},{1,9},{9,1},{2,10},{10,2},{3,11},{11,3},{4,12},{12,4},... | collective-permute-start | bytes 1572872 | tf_op jit(solution)/shard_map/ppermute | solution.py:582
  28.2 0.9 %shard_map.155 = (bf16[2,3,48,192]{3,2,1,0:T(8,128)(2,1)S(1)}, bf16[64,8,128]{2,1,0:T(8,128)(2,1)S(1)}, bf16[32,128]{1,0:T(8,128)(2,1)S(1)}) custom-call(bf16[4,576,144]{2,1,0:T(8,128)(2,1)S(1)} %get-tuple-element.36.dp_t, f32[576,192]{1,0:T(8,128)S(1)} %get-tuple-element.37.hid, f32[2,648,128]{2,1,0:T(8,128)S(1)} %get-tuple-element.38.xs, ...), custom_call_target="tpu_custom_call" | custom-call | tf_op jit(solution)/shard_map/pallas_call | solution.py:553
  29.2 0.6 collective-permute-done.3.got_ref
  29.8 0.1 shard_map.156
  29.9 19.1 %all_to_all.10.got_ref = bf16[64,40,128]{2,1,0:T(8,128)(2,1)S(1)} all-to-all(bf16[64,40,128]{2,1,0:T(8,128)(2,1)S(1)} %shard_map.156), channel_id=1, replica_groups=mesh['y'=4,'zh'=2,'c'=2,'zl'=2,'x'=4] {'y','zh','zl','x'}, dimensions={0} | all-to-all | bytes 1310720 | tf_op jit(solution)/shard_map/all_to_all | solution.py:592
  49.0 0.1 shard_map.157
  49.1 16.9 %all_to_all.11.a_ref = bf16[64,40,128]{2,1,0:T(8,128)(2,1)S(1)} all-to-all(bf16[64,40,128]{2,1,0:T(8,128)(2,1)S(1)} %shard_map.157), channel_id=1, replica_groups=mesh['y'=4,'zh'=2,'c'=2,'zl'=2,'x'=4] {'y','zh','zl','x'}, dimensions={0} | all-to-all | bytes 1310720 | tf_op jit(solution)/shard_map/all_to_all | solution.py:600
  66.1 3.1 %collective-permute-start.4 = (bf16[64,40,128]{2,1,0:T(8,128)(2,1)S(1)}, bf16[64,40,128]{2,1,0:T(8,128)(2,1)S(1)}, u32[]{:S(2)}, u32[]{:S(2)}) collective-permute-start(bf16[64,40,128]{2,1,0:T(8,128)(2,1)S(1)} %all_to_all.11.a_ref), channel_id=1, source_target_pairs={{0,8},{8,0},{1,9},{9,1},{2,10},{10,2},{3,11},{11,3},{4,12},{12,4},... | collective-permute-start | bytes 1966088 | tf_op jit(solution)/shard_map/ppermute | solution.py:601
  69.1 1.7 %collective-permute-done.4.b_ref = bf16[64,40,128]{2,1,0:T(8,128)(2,1)S(1)} collective-permute-done((bf16[64,40,128]{2,1,0:T(8,128)(2,1)S(1)}, bf16[64,40,128]{2,1,0:T(8,128)(2,1)S(1)}, u32[]{:S(2)}, u32[]{:S(2)}) %collective-permute-start.4) | collective-permute-done | bytes 655392 | tf_op jit(solution)/shard_map/ppermute | solution.py:601
  70.9 1.7 %shard_map.158 = (bf16[2,6,48,192]{3,2,1,0:T(8,128)(2,1)}, f32[1,192]{1,0:T(1,128)}, f32[192,576]{1,0:T(8,128)}, f32[192,192]{1,0:T(8,128)}, f32[1,192]{1,0:T(1,...) custom-call(bf16[64,40,128]{2,1,0:T(8,128)(2,1)S(1)} %all_to_all.11.a_ref, ...), custom_call_target="tpu_custom_call" | custom-call | tf_op jit(solution)/shard_map/pallas_call | solution.py:604
  (6 shorter events, 0.0 us)
Async XLA Ops:
  0.6 12.1 %copy-start.5 = (f32[192]{0:T(256)S(1)}, f32[192]{0:T(256)}, u32[]{:S(2)}) copy-start(f32[192]{0:T(256)} %param.14) | copy-start | bytes 2308
  0.6 12.1 %copy-start.6 = (f32[192]{0:T(256)S(1)}, f32[192]{0:T(256)}, u32[]{:S(2)}) copy-start(f32[192]{0:T(256)} %param.11) | copy-start | bytes 2308
  0.7 12.2 %copy-start.4 = (f32[1,6,3312]{2,0,1:T(1,128)S(1)}, f32[1,6,3312]{2,0,1:T(1,128)}, u32[]{:S(2)}) copy-start(f32[1,6,3312]{2,0,1:T(1,128)} %param.17) | copy-start | bytes 238468
  0.7 12.3 %copy-start.1 = (bf16[768,192]{0,1:T(8,128)(2,1)S(1)}, bf16[768,192]{0,1:T(8,128)(2,1)}, u32[]{:S(2)}) copy-start(bf16[768,192]{0,1:T(8,128)(2,1)} %param.16) | copy-start | bytes 884740
  0.7 12.3 %copy-start = (bf16[192,768]{1,0:T(8,128)(2,1)S(1)}, bf16[192,768]{1,0:T(8,128)(2,1)}, u32[]{:S(2)}) copy-start(bf16[192,768]{1,0:T(8,128)(2,1)} %param.15) | copy-start | bytes 884740
  0.7 12.3 %copy-start.3 = (bf16[192,192]{1,0:T(8,128)(2,1)S(1)}, bf16[192,192]{1,0:T(8,128)(2,1)}, u32[]{:S(2)}) copy-start(bf16[192,192]{1,0:T(8,128)(2,1)} %param.13) | copy-start | bytes 221188
  0.7 12.3 %copy-start.2 = (bf16[192,576]{1,0:T(8,128)(2,1)S(1)}, bf16[192,576]{1,0:T(8,128)(2,1)}, u32[]{:S(2)}) copy-start(bf16[192,576]{1,0:T(8,128)(2,1)} %param.12) | copy-start | bytes 663556
  2.1 12.4 %collective-permute-start.1 = (bf16[2,3,3,6,128]{4,3,2,1,0:T(8,128)(2,1)S(1)}, bf16[2,3,3,6,128]{4,3,2,1,0:T(8,128)(2,1)S(1)}, u32[]{:S(2)}, u32[]{:S(2)}) collective-permute-start(bf16[2,3,3,6,128]{4,3,2,1,0:T(8,128)(2,1)S(1)} %get-tuple-element.30), channel_id=1, source_target_pairs={{0,120},{8,0},{16,8},{24,16},{32,24},{40,32},{48,40},{56,48},{64,5... | collective-permute-start | bytes 82952 | tf_op jit(solution)/shard_map/ppermute | solution.py:572
  3.5 10.9 %collective-permute-start.2 = (bf16[2,3,3,6,128]{4,3,2,1,0:T(8,128)(2,1)S(1)}, bf16[2,3,3,6,128]{4,3,2,1,0:T(8,128)(2,1)S(1)}, u32[]{:S(2)}, u32[]{:S(2)}) collective-permute-start(bf16[2,3,3,6,128]{4,3,2,1,0:T(8,128)(2,1)S(1)} %get-tuple-element.31), channel_id=1, source_target_pairs={{0,127},{1,120},{2,121},{3,122},{4,123},{5,124},{6,125},{7,126},{8... | collective-permute-start | bytes 82952 | tf_op jit(solution)/shard_map/ppermute | solution.py:573
  12.2 6.3 %collective-permute-start = (bf16[2,3,128,128]{3,2,1,0:T(8,128)(2,1)S(1)}, bf16[2,3,128,128]{3,2,1,0:T(8,128)(2,1)S(1)}, u32[]{:S(2)}, u32[]{:S(2)}) collective-permute-start(bf16[2,3,128,128]{3,2,1,0:T(8,128)(2,1)S(1)} %get-tuple-element.29), channel_id=1, source_target_pairs={{0,7},{1,0},{2,1},{3,2},{4,3},{5,4},{6,5},{7,6},{8,15},{9,8},{10,9... | collective-permute-start | bytes 589832 | tf_op jit(solution)/shard_map/ppermute | solution.py:571
  27.1 2.6 %collective-permute-start.3 = (bf16[64,32,128]{2,1,0:T(8,128)(2,1)S(1)}, bf16[64,32,128]{2,1,0:T(8,128)(2,1)S(1)}, u32[]{:S(2)}, u32[]{:S(2)}) collective-permute-start(bf16[64,32,128]{2,1,0:T(8,128)(2,1)S(1)} %get-tuple-element.35), channel_id=1, source_target_pairs={{0,8},{8,0},{1,9},{9,1},{2,10},{10,2},{3,11},{11,3},{4,12},{12,4},... | collective-permute-start | bytes 1572872 | tf_op jit(solution)/shard_map/ppermute | solution.py:582
  66.1 4.8 %collective-permute-start.4 = (bf16[64,40,128]{2,1,0:T(8,128)(2,1)S(1)}, bf16[64,40,128]{2,1,0:T(8,128)(2,1)S(1)}, u32[]{:S(2)}, u32[]{:S(2)}) collective-permute-start(bf16[64,40,128]{2,1,0:T(8,128)(2,1)S(1)} %all_to_all.11.a_ref), channel_id=1, source_target_pairs={{0,8},{8,0},{1,9},{9,1},{2,10},{10,2},{3,11},{11,3},{4,12},{12,4},... | collective-permute-start | bytes 1966088 | tf_op jit(solution)/shard_map/ppermute | solution.py:601

commit v2 on v1

--- a/solution.py
+++ b/solution.py
@@ -410,16 +410,25 @@
 def finish_kernel(
     a_ref, b_ref, own_ref,
     dx_ref, dg1_ref, dqkv_ref, dproj_ref, dg2_ref, dup_ref, ddown_ref, dt_ref,
-    m_acc, table, g_acc, line, lines, flat, grad_scale,
+    table, g_acc, line, lines, flat, grad_scale,
 ):
     core = lax.axis_index("c")
-    a_half = pl.multiple_of(core * 288, 32)
-    b_half = pl.multiple_of((1 - core) * 288, 32)
-    for i in range(9):
+    for block in range(18):
+        mine = core == block // 9
+        tiles = []
         for b in range(6):
-            cols = slice(b * 128, (b + 1) * 128)
-            m_acc[pl.ds(a_half + 32 * i, 32), cols] = a_ref[i * 6 + b, :32].astype(F32) * grad_scale
-            m_acc[pl.ds(b_half + 32 * i, 32), cols] = b_ref[i * 6 + b, :32].astype(F32) * grad_scale
+            chunk = block % 9 * 6 + b
+            tiles.append(jnp.where(mine, a_ref[chunk, :32].astype(F32), b_ref[chunk, :32].astype(F32)) * grad_scale)
+        rows = slice(block % 6 * 32, block % 6 * 32 + 32)
+        if block < 6:
+            for b in range(4):
+                dqkv_ref[rows, b * 128 : (b + 1) * 128] = tiles[b]
+            dqkv_ref[rows, 512:] = tiles[4][:, :64]
+            dproj_ref[rows, :] = jnp.concatenate((tiles[4][:, 64:], tiles[5]), axis=1)
+        else:
+            out = dup_ref if block < 12 else ddown_ref
+            for b in range(6):
+                out[rows, b * 128 : (b + 1) * 128] = tiles[b]
     for ref, half in ((a_ref, core), (b_ref, 1 - core)):
 
         @pl.when(half == 0)
@@ -434,10 +443,6 @@
             for k in range(5, 9):
                 table[k % 3, 32 * (k // 3) : 32 * (k // 3) + 32, :] = ref[W_CHUNKS + k - 5, :32].astype(F32)
 
-    dqkv_ref[...] = m_acc[:D, : 3 * D]
-    dproj_ref[...] = m_acc[:D, 3 * D :]
-    dup_ref[...] = m_acc[D : 2 * D, :]
-    ddown_ref[...] = m_acc[2 * D :, :]
     d_gain = (a_ref[GAIN_AT, :32].astype(F32) + b_ref[GAIN_AT, :32].astype(F32)) * grad_scale
     dg1_ref[:, :128] = d_gain[0:1, :]
     dg1_ref[:, 128:] = d_gain[1:2, : D - 128]
@@ -616,7 +621,6 @@
         in_specs=[vmem_spec()] * 3,
         out_specs=[vmem_spec()] * 8,
         scratch_shapes=[
-            pltpu.VMEM((3 * D, MLP), F32),
             pltpu.VMEM((3, 8 * RA, 128), F32),
             pltpu.VMEM((32, 256), F32),
             pltpu.VMEM((COLS, D), F32),

time: 72.8 us -> 72.8 us (level)
  no operation moved by 1% of the time
where the time goes in v2:
time: 72.8 us; the launch traced here: 72.6 us
  blocking collectives  36 us (49%)
  starting transfers between devices  14.9 us (20%)
  Pallas kernels  12.8 us (18%)
  waiting for transfers between devices  6.35 us (9%)
  other arithmetic  1.34 us (2%)
  between operations  0.81 us (1%)
    all_to_all x1, blocking collectives, local(): spread = lax.all_to_all(joined, CHIPS, 0, 0, tiled=True)  19.1 us
    all_to_all x1, blocking collectives, local(): half_a = lax.all_to_all(reply, CHIPS, 0, 0, tiled=True)  16.9 us
    ppermute x1, starting transfers between devices, local(): nc = lax.ppermute(part_c, LON + LAT, shift_pairs(-1, -1))  8.67 us
    pallas_call x1, Pallas kernels, run_block(): pl.pallas_call(block_kernel, out_shape=(shape((64, 32, 128), BF), shape((...  8.63 us
    ppermute x1, waiting for transfers between devices, local(): na = lax.ppermute(part_a, LAT, one_axis(8, -1))  4.01 us
    ppermute x1, starting transfers between devices, local(): half_b = lax.ppermute(half_a, 'c', pair)  3.07 us
    ppermute x1, waiting for transfers between devices, local(): half_b = lax.ppermute(half_a, 'c', pair)  1.72 us
    pallas_call x1, Pallas kernels, local(): pl.pallas_call(functools.partial(finish_kernel, grad_scale=1.0 / math.sqr...  1.71 us
  transfers between devices with their start and end apart: 5, of which 3 were waited for; matrix products, arithmetic and copies ran while one was open for 1% of the time, Pallas kernels for 3%

profile of v2, /device:TPU:1, one launch (start us, length us, event | category | flops | bytes accessed | tf_op | source)
XLA Modules:
  0.0 72.6 jit_solution(7582768357462271482)
XLA Ops:
  0.6 0.0 copy-start.5
  0.6 0.0 copy-start.6
  0.7 0.0 copy-start.4
  0.7 0.0 copy-start.1
  0.7 0.0 copy-start
  0.7 1.2 %pad_add_fusion.both_ref = bf16[4,6,48,192]{3,2,1,0:T(8,128)(2,1)S(1)} fusion(bf16[2,6,48,192]{3,2,1,0:T(8,128)(2,1)} %param.10, bf16[2,6,48,192]{3,2,1,0:T(8,128)(2,1)} %param.9), kind=kLoop, calls=%fused_computation | loop fusion | flops 221184 | bytes 884736 | tf_op jit(solution)/shard_map/add | solution.py:574
  1.9 0.1 shard_map.152
  2.1 1.5 %collective-permute-start.1 = (bf16[2,3,3,6,128]{4,3,2,1,0:T(8,128)(2,1)S(1)}, bf16[2,3,3,6,128]{4,3,2,1,0:T(8,128)(2,1)S(1)}, u32[]{:S(2)}, u32[]{:S(2)}) collective-permute-start(bf16[2,3,3,6,128]{4,3,2,1,0:T(8,128)(2,1)S(1)} %get-tuple-element.30), channel_id=1, source_target_pairs={{0,120},{8,0},{16,8},{24,16},{32,24},{40,32},{48,40},{56,48},{64,5... | collective-permute-start | bytes 82952 | tf_op jit(solution)/shard_map/ppermute | solution.py:577
  3.5 8.7 %collective-permute-start.2 = (bf16[2,3,3,6,128]{4,3,2,1,0:T(8,128)(2,1)S(1)}, bf16[2,3,3,6,128]{4,3,2,1,0:T(8,128)(2,1)S(1)}, u32[]{:S(2)}, u32[]{:S(2)}) collective-permute-start(bf16[2,3,3,6,128]{4,3,2,1,0:T(8,128)(2,1)S(1)} %get-tuple-element.31), channel_id=1, source_target_pairs={{0,127},{1,120},{2,121},{3,122},{4,123},{5,124},{6,125},{7,126},{8... | collective-permute-start | bytes 82952 | tf_op jit(solution)/shard_map/ppermute | solution.py:578
  12.2 0.5 collective-permute-start
  12.8 0.0 copy-done.4
  12.8 0.1 pad_maximum_fusion.table_ref
  12.9 0.0 copy-done.1
  12.9 0.0 copy-done
  12.9 0.0 copy-done.3
  13.0 0.0 copy-done.2
  13.0 0.3 concatenate.6.w_ref
  13.3 1.2 %shard_map.153 = (f32[6,144,144]{2,1,0:T(8,128)S(1)}, bf16[576,192]{1,0:T(8,128)(2,1)S(1)}) custom-call(f32[8,1,3312]{2,1,0:T(1,128)S(1)} %pad_maximum_fusion.table_ref, bf16[192,2304]{1,0:T(8,128)(2,1)S(1)} %concatenate.6.w_ref), custom_call_target="tpu_custom_call" | custom-call | tf_op jit(solution)/shard_map/pallas_call | solution.py:495
  14.5 0.0 collective-permute-done.1.nb_ref
  14.5 0.0 collective-permute-done.2.nc_ref
  14.5 4.0 %collective-permute-done.na_ref = bf16[2,3,128,128]{3,2,1,0:T(8,128)(2,1)S(1)} collective-permute-done((bf16[2,3,128,128]{3,2,1,0:T(8,128)(2,1)S(1)}, bf16[2,3,128,128]{3,2,1,0:T(8,128)(2,1)S(1)}, u32[]{:S(2)}, u32[]{:S(2)}) %collective-permute-start) | collective-permute-done | bytes 196640 | tf_op jit(solution)/shard_map/ppermute | solution.py:576
  18.5 8.6 %shard_map.154 = (bf16[64,32,128]{2,1,0:T(8,128)(2,1)S(1)}, bf16[64,32,128]{2,1,0:T(8,128)(2,1)S(1)}, bf16[4,576,144]{2,1,0:T(8,128)(2,1)S(1)}, f32[576,192]{1,0:T(8,128)S(1)}, f32[2,648,128]{2,1,0:T(8,128)S(1)}) custom-call(bf16[4,6,48,192]{3,2,1,0:T(8,128)(2,1)S(1)} %pad_add_fusion.both_ref, bf16[2,3,128,128]{3,2,1,0:T(8,128)(2,1)S(1)} %collective-permute-done.na_ref, ...), custom_call_target="tpu_custom_call" | custom-call | tf_op jit(solution)/shard_map/pallas_call | solution.py:526
  27.1 1.1 %collective-permute-start.3 = (bf16[64,32,128]{2,1,0:T(8,128)(2,1)S(1)}, bf16[64,32,128]{2,1,0:T(8,128)(2,1)S(1)}, u32[]{:S(2)}, u32[]{:S(2)}) collective-permute-start(bf16[64,32,128]{2,1,0:T(8,128)(2,1)S(1)} %get-tuple-element.35), channel_id=1, source_target_pairs={{0,8},{8,0},{1,9},{9,1},{2,10},{10,2},{3,11},{11,3},{4,12},{12,4},... | collective-permute-start | bytes 1572872 | tf_op jit(solution)/shard_map/ppermute | solution.py:587
  28.2 0.9 %shard_map.155 = (bf16[2,3,48,192]{3,2,1,0:T(8,128)(2,1)S(1)}, bf16[64,8,128]{2,1,0:T(8,128)(2,1)S(1)}, bf16[32,128]{1,0:T(8,128)(2,1)S(1)}) custom-call(bf16[4,576,144]{2,1,0:T(8,128)(2,1)S(1)} %get-tuple-element.36.dp_t, f32[576,192]{1,0:T(8,128)S(1)} %get-tuple-element.37.hid, f32[2,648,128]{2,1,0:T(8,128)S(1)} %get-tuple-element.38.xs, ...), custom_call_target="tpu_custom_call" | custom-call | tf_op jit(solution)/shard_map/pallas_call | solution.py:558
  29.2 0.6 collective-permute-done.3.got_ref
  29.8 0.1 shard_map.156
  29.9 19.1 %all_to_all.10.got_ref = bf16[64,40,128]{2,1,0:T(8,128)(2,1)S(1)} all-to-all(bf16[64,40,128]{2,1,0:T(8,128)(2,1)S(1)} %shard_map.156), channel_id=1, replica_groups=mesh['y'=4,'zh'=2,'c'=2,'zl'=2,'x'=4] {'y','zh','zl','x'}, dimensions={0} | all-to-all | bytes 1310720 | tf_op jit(solution)/shard_map/all_to_all | solution.py:597
  49.0 0.1 shard_map.157
  49.1 16.9 %all_to_all.11.a_ref = bf16[64,40,128]{2,1,0:T(8,128)(2,1)S(1)} all-to-all(bf16[64,40,128]{2,1,0:T(8,128)(2,1)S(1)} %shard_map.157), channel_id=1, replica_groups=mesh['y'=4,'zh'=2,'c'=2,'zl'=2,'x'=4] {'y','zh','zl','x'}, dimensions={0} | all-to-all | bytes 1310720 | tf_op jit(solution)/shard_map/all_to_all | solution.py:605
  66.1 3.1 %collective-permute-start.4 = (bf16[64,40,128]{2,1,0:T(8,128)(2,1)S(1)}, bf16[64,40,128]{2,1,0:T(8,128)(2,1)S(1)}, u32[]{:S(2)}, u32[]{:S(2)}) collective-permute-start(bf16[64,40,128]{2,1,0:T(8,128)(2,1)S(1)} %all_to_all.11.a_ref), channel_id=1, source_target_pairs={{0,8},{8,0},{1,9},{9,1},{2,10},{10,2},{3,11},{11,3},{4,12},{12,4},... | collective-permute-start | bytes 1966088 | tf_op jit(solution)/shard_map/ppermute | solution.py:606
  69.1 1.7 %collective-permute-done.4.b_ref = bf16[64,40,128]{2,1,0:T(8,128)(2,1)S(1)} collective-permute-done((bf16[64,40,128]{2,1,0:T(8,128)(2,1)S(1)}, bf16[64,40,128]{2,1,0:T(8,128)(2,1)S(1)}, u32[]{:S(2)}, u32[]{:S(2)}) %collective-permute-start.4) | collective-permute-done | bytes 655392 | tf_op jit(solution)/shard_map/ppermute | solution.py:606
  70.9 1.7 %shard_map.158 = (bf16[2,6,48,192]{3,2,1,0:T(8,128)(2,1)}, f32[1,192]{1,0:T(1,128)}, f32[192,576]{1,0:T(8,128)}, f32[192,192]{1,0:T(8,128)}, f32[1,192]{1,0:T(1,...) custom-call(bf16[64,40,128]{2,1,0:T(8,128)(2,1)S(1)} %all_to_all.11.a_ref, ...), custom_call_target="tpu_custom_call" | custom-call | tf_op jit(solution)/shard_map/pallas_call | solution.py:609
  (6 shorter events, 0.0 us)
Async XLA Ops:
  0.6 12.1 %copy-start.5 = (f32[192]{0:T(256)S(1)}, f32[192]{0:T(256)}, u32[]{:S(2)}) copy-start(f32[192]{0:T(256)} %param.14) | copy-start | bytes 2308
  0.6 12.1 %copy-start.6 = (f32[192]{0:T(256)S(1)}, f32[192]{0:T(256)}, u32[]{:S(2)}) copy-start(f32[192]{0:T(256)} %param.11) | copy-start | bytes 2308
  0.7 12.2 %copy-start.4 = (f32[1,6,3312]{2,0,1:T(1,128)S(1)}, f32[1,6,3312]{2,0,1:T(1,128)}, u32[]{:S(2)}) copy-start(f32[1,6,3312]{2,0,1:T(1,128)} %param.17) | copy-start | bytes 238468
  0.7 12.3 %copy-start.1 = (bf16[768,192]{0,1:T(8,128)(2,1)S(1)}, bf16[768,192]{0,1:T(8,128)(2,1)}, u32[]{:S(2)}) copy-start(bf16[768,192]{0,1:T(8,128)(2,1)} %param.16) | copy-start | bytes 884740
  0.7 12.3 %copy-start = (bf16[192,768]{1,0:T(8,128)(2,1)S(1)}, bf16[192,768]{1,0:T(8,128)(2,1)}, u32[]{:S(2)}) copy-start(bf16[192,768]{1,0:T(8,128)(2,1)} %param.15) | copy-start | bytes 884740
  0.7 12.3 %copy-start.3 = (bf16[192,192]{1,0:T(8,128)(2,1)S(1)}, bf16[192,192]{1,0:T(8,128)(2,1)}, u32[]{:S(2)}) copy-start(bf16[192,192]{1,0:T(8,128)(2,1)} %param.13) | copy-start | bytes 221188
  0.7 12.3 %copy-start.2 = (bf16[192,576]{1,0:T(8,128)(2,1)S(1)}, bf16[192,576]{1,0:T(8,128)(2,1)}, u32[]{:S(2)}) copy-start(bf16[192,576]{1,0:T(8,128)(2,1)} %param.12) | copy-start | bytes 663556
  2.1 12.4 %collective-permute-start.1 = (bf16[2,3,3,6,128]{4,3,2,1,0:T(8,128)(2,1)S(1)}, bf16[2,3,3,6,128]{4,3,2,1,0:T(8,128)(2,1)S(1)}, u32[]{:S(2)}, u32[]{:S(2)}) collective-permute-start(bf16[2,3,3,6,128]{4,3,2,1,0:T(8,128)(2,1)S(1)} %get-tuple-element.30), channel_id=1, source_target_pairs={{0,120},{8,0},{16,8},{24,16},{32,24},{40,32},{48,40},{56,48},{64,5... | collective-permute-start | bytes 82952 | tf_op jit(solution)/shard_map/ppermute | solution.py:577
  3.5 10.9 %collective-permute-start.2 = (bf16[2,3,3,6,128]{4,3,2,1,0:T(8,128)(2,1)S(1)}, bf16[2,3,3,6,128]{4,3,2,1,0:T(8,128)(2,1)S(1)}, u32[]{:S(2)}, u32[]{:S(2)}) collective-permute-start(bf16[2,3,3,6,128]{4,3,2,1,0:T(8,128)(2,1)S(1)} %get-tuple-element.31), channel_id=1, source_target_pairs={{0,127},{1,120},{2,121},{3,122},{4,123},{5,124},{6,125},{7,126},{8... | collective-permute-start | bytes 82952 | tf_op jit(solution)/shard_map/ppermute | solution.py:578
  12.2 6.3 %collective-permute-start = (bf16[2,3,128,128]{3,2,1,0:T(8,128)(2,1)S(1)}, bf16[2,3,128,128]{3,2,1,0:T(8,128)(2,1)S(1)}, u32[]{:S(2)}, u32[]{:S(2)}) collective-permute-start(bf16[2,3,128,128]{3,2,1,0:T(8,128)(2,1)S(1)} %get-tuple-element.29), channel_id=1, source_target_pairs={{0,7},{1,0},{2,1},{3,2},{4,3},{5,4},{6,5},{7,6},{8,15},{9,8},{10,9... | collective-permute-start | bytes 589832 | tf_op jit(solution)/shard_map/ppermute | solution.py:576
  27.1 2.6 %collective-permute-start.3 = (bf16[64,32,128]{2,1,0:T(8,128)(2,1)S(1)}, bf16[64,32,128]{2,1,0:T(8,128)(2,1)S(1)}, u32[]{:S(2)}, u32[]{:S(2)}) collective-permute-start(bf16[64,32,128]{2,1,0:T(8,128)(2,1)S(1)} %get-tuple-element.35), channel_id=1, source_target_pairs={{0,8},{8,0},{1,9},{9,1},{2,10},{10,2},{3,11},{11,3},{4,12},{12,4},... | collective-permute-start | bytes 1572872 | tf_op jit(solution)/shard_map/ppermute | solution.py:587
  66.1 4.8 %collective-permute-start.4 = (bf16[64,40,128]{2,1,0:T(8,128)(2,1)S(1)}, bf16[64,40,128]{2,1,0:T(8,128)(2,1)S(1)}, u32[]{:S(2)}, u32[]{:S(2)}) collective-permute-start(bf16[64,40,128]{2,1,0:T(8,128)(2,1)S(1)} %all_to_all.11.a_ref), channel_id=1, source_target_pairs={{0,8},{8,0},{1,9},{9,1},{2,10},{10,2},{3,11},{11,3},{4,12},{12,4},... | collective-permute-start | bytes 1966088 | tf_op jit(solution)/shard_map/ppermute | solution.py:606

commit v3 on v2

--- a/solution.py
+++ b/solution.py
@@ -55,13 +55,6 @@
 
 def tn(a, b):
     return lax.dot_general(a, b, (((0,), (0,)), ((), ())), preferred_element_type=F32)
-
-
-def put_rows(dst, start, count, rows):
-    rows = rows.astype(F32)
-    spare = jnp.zeros((count, 256 - D), F32)
-    dst[0, pl.ds(start, count, stride=RA), :] = rows[:, :128]
-    dst[1, pl.ds(start, count, stride=RA), :] = jnp.concatenate((rows[:, 128:], spare), axis=1)
 
 
 def put_parts(xs, ys, start, count, parts):
@@ -204,15 +197,16 @@
 ):
     for l in range(2):
         for r in range(HALF_LAT):
-            put_rows(xs, l * 6 + r, COLS, both_ref[l, r + HALF_LAT])
-            put_rows(ys, l * 6 + r, COLS, both_ref[2 + l, r + HALF_LAT])
+            x = both_ref[l, r + HALF_LAT].astype(F32)
+            dy = both_ref[2 + l, r + HALF_LAT].astype(F32)
+            pair = jnp.concatenate((x[:, 128:], dy[:, 128:]), axis=1)
+            put_parts(xs, ys, l * 6 + r, COLS, (x[:, :128], dy[:, :128], pair))
             north = na_ref[l, r].astype(F32)
             north = [north[k * INNER : (k + 1) * INNER] for k in range(3)]
             put_parts(xs, ys, HALF_LON * RA + l * 6 + r + HALF_LAT, INNER, north)
             put_pair(xs, ys, COLS * RA + l * 6 + r, HALF_LON, nb_ref, l, r)
             put_pair(xs, ys, COLS * RA + l * 6 + r + HALF_LAT, HALF_LON, nc_ref, l, r)
 
-    d_bias[...] = jnp.zeros_like(d_bias)
     g_acc[...] = jnp.zeros_like(g_acc)
 
     g1 = table_ref[HEADS][:, :D]
@@ -284,7 +278,7 @@
             pf = probs[w, h].astype(F32)
             prod = pf * d_probs[k]
             ds = prod - pf * jnp.sum(prod, axis=0, keepdims=True)
-            d_bias[h] = d_bias[h] + ds
+            d_bias[h] = ds if w == 0 else d_bias[h] + ds
             dss[k] = ds.astype(BF)
         for k, (w, h) in enumerate(jobs):
             part = parts[h]

time: 72.8 us -> 72.6 us (level)
  no operation moved by 1% of the time
where the time goes in v3:
time: 72.6 us; the launch traced here: 72.4 us
  blocking collectives  36 us (50%)
  starting transfers between devices  14.9 us (21%)
  Pallas kernels  12.7 us (17%)
  waiting for transfers between devices  6.35 us (9%)
  other arithmetic  1.34 us (2%)
  between operations  0.81 us (1%)
    all_to_all x1, blocking collectives, local(): spread = lax.all_to_all(joined, CHIPS, 0, 0, tiled=True)  19.1 us
    all_to_all x1, blocking collectives, local(): half_a = lax.all_to_all(reply, CHIPS, 0, 0, tiled=True)  16.9 us
    ppermute x1, starting transfers between devices, local(): nc = lax.ppermute(part_c, LON + LAT, shift_pairs(-1, -1))  8.67 us
    pallas_call x1, Pallas kernels, run_block(): pl.pallas_call(block_kernel, out_shape=(shape((64, 32, 128), BF), shape((...  8.47 us
    ppermute x1, waiting for transfers between devices, local(): na = lax.ppermute(part_a, LAT, one_axis(8, -1))  4.01 us
    ppermute x1, starting transfers between devices, local(): half_b = lax.ppermute(half_a, 'c', pair)  3.07 us
    ppermute x1, waiting for transfers between devices, local(): half_b = lax.ppermute(half_a, 'c', pair)  1.72 us
    pallas_call x1, Pallas kernels, local(): pl.pallas_call(functools.partial(finish_kernel, grad_scale=1.0 / math.sqr...  1.71 us
  transfers between devices with their start and end apart: 5, of which 3 were waited for; matrix products, arithmetic and copies ran while one was open for 1% of the time, Pallas kernels for 3%

profile of v3, /device:TPU:1, one launch (start us, length us, event | category | flops | bytes accessed | tf_op | source)
XLA Modules:
  0.0 72.4 jit_solution(16599428381436816708)
XLA Ops:
  0.6 0.0 copy-start.5
  0.6 0.0 copy-start.6
  0.7 0.0 copy-start.4
  0.7 0.0 copy-start.1
  0.7 0.0 copy-start
  0.7 1.2 %pad_add_fusion.both_ref = bf16[4,6,48,192]{3,2,1,0:T(8,128)(2,1)S(1)} fusion(bf16[2,6,48,192]{3,2,1,0:T(8,128)(2,1)} %param.10, bf16[2,6,48,192]{3,2,1,0:T(8,128)(2,1)} %param.9), kind=kLoop, calls=%fused_computation | loop fusion | flops 221184 | bytes 884736 | tf_op jit(solution)/shard_map/add | solution.py:568
  1.9 0.1 shard_map.152
  2.1 1.5 %collective-permute-start.1 = (bf16[2,3,3,6,128]{4,3,2,1,0:T(8,128)(2,1)S(1)}, bf16[2,3,3,6,128]{4,3,2,1,0:T(8,128)(2,1)S(1)}, u32[]{:S(2)}, u32[]{:S(2)}) collective-permute-start(bf16[2,3,3,6,128]{4,3,2,1,0:T(8,128)(2,1)S(1)} %get-tuple-element.30), channel_id=1, source_target_pairs={{0,120},{8,0},{16,8},{24,16},{32,24},{40,32},{48,40},{56,48},{64,5... | collective-permute-start | bytes 82952 | tf_op jit(solution)/shard_map/ppermute | solution.py:571
  3.5 8.7 %collective-permute-start.2 = (bf16[2,3,3,6,128]{4,3,2,1,0:T(8,128)(2,1)S(1)}, bf16[2,3,3,6,128]{4,3,2,1,0:T(8,128)(2,1)S(1)}, u32[]{:S(2)}, u32[]{:S(2)}) collective-permute-start(bf16[2,3,3,6,128]{4,3,2,1,0:T(8,128)(2,1)S(1)} %get-tuple-element.31), channel_id=1, source_target_pairs={{0,127},{1,120},{2,121},{3,122},{4,123},{5,124},{6,125},{7,126},{8... | collective-permute-start | bytes 82952 | tf_op jit(solution)/shard_map/ppermute | solution.py:572
  12.2 0.5 collective-permute-start
  12.8 0.0 copy-done.4
  12.8 0.1 pad_maximum_fusion.table_ref
  12.9 0.0 copy-done.1
  12.9 0.0 copy-done
  12.9 0.0 copy-done.3
  13.0 0.0 copy-done.2
  13.0 0.3 concatenate.6.w_ref
  13.3 1.2 %shard_map.153 = (f32[6,144,144]{2,1,0:T(8,128)S(1)}, bf16[576,192]{1,0:T(8,128)(2,1)S(1)}) custom-call(f32[8,1,3312]{2,1,0:T(1,128)S(1)} %pad_maximum_fusion.table_ref, bf16[192,2304]{1,0:T(8,128)(2,1)S(1)} %concatenate.6.w_ref), custom_call_target="tpu_custom_call" | custom-call | tf_op jit(solution)/shard_map/pallas_call | solution.py:489
  14.5 0.0 collective-permute-done.1.nb_ref
  14.5 0.0 collective-permute-done.2.nc_ref
  14.5 4.0 %collective-permute-done.na_ref = bf16[2,3,128,128]{3,2,1,0:T(8,128)(2,1)S(1)} collective-permute-done((bf16[2,3,128,128]{3,2,1,0:T(8,128)(2,1)S(1)}, bf16[2,3,128,128]{3,2,1,0:T(8,128)(2,1)S(1)}, u32[]{:S(2)}, u32[]{:S(2)}) %collective-permute-start) | collective-permute-done | bytes 196640 | tf_op jit(solution)/shard_map/ppermute | solution.py:570
  18.5 8.5 %shard_map.154 = (bf16[64,32,128]{2,1,0:T(8,128)(2,1)S(1)}, bf16[64,32,128]{2,1,0:T(8,128)(2,1)S(1)}, bf16[4,576,144]{2,1,0:T(8,128)(2,1)S(1)}, f32[576,192]{1,0:T(8,128)S(1)}, f32[2,648,128]{2,1,0:T(8,128)S(1)}) custom-call(bf16[4,6,48,192]{3,2,1,0:T(8,128)(2,1)S(1)} %pad_add_fusion.both_ref, bf16[2,3,128,128]{3,2,1,0:T(8,128)(2,1)S(1)} %collective-permute-done.na_ref, ...), custom_call_target="tpu_custom_call" | custom-call | tf_op jit(solution)/shard_map/pallas_call | solution.py:520
  27.0 1.1 %collective-permute-start.3 = (bf16[64,32,128]{2,1,0:T(8,128)(2,1)S(1)}, bf16[64,32,128]{2,1,0:T(8,128)(2,1)S(1)}, u32[]{:S(2)}, u32[]{:S(2)}) collective-permute-start(bf16[64,32,128]{2,1,0:T(8,128)(2,1)S(1)} %get-tuple-element.35), channel_id=1, source_target_pairs={{0,8},{8,0},{1,9},{9,1},{2,10},{10,2},{3,11},{11,3},{4,12},{12,4},... | collective-permute-start | bytes 1572872 | tf_op jit(solution)/shard_map/ppermute | solution.py:581
  28.1 0.9 %shard_map.155 = (bf16[2,3,48,192]{3,2,1,0:T(8,128)(2,1)S(1)}, bf16[64,8,128]{2,1,0:T(8,128)(2,1)S(1)}, bf16[32,128]{1,0:T(8,128)(2,1)S(1)}) custom-call(bf16[4,576,144]{2,1,0:T(8,128)(2,1)S(1)} %get-tuple-element.36.dp_t, f32[576,192]{1,0:T(8,128)S(1)} %get-tuple-element.37.hid, f32[2,648,128]{2,1,0:T(8,128)S(1)} %get-tuple-element.38.xs, ...), custom_call_target="tpu_custom_call" | custom-call | tf_op jit(solution)/shard_map/pallas_call | solution.py:552
  29.0 0.6 collective-permute-done.3.got_ref
  29.6 0.1 shard_map.156
  29.8 19.1 %all_to_all.10.got_ref = bf16[64,40,128]{2,1,0:T(8,128)(2,1)S(1)} all-to-all(bf16[64,40,128]{2,1,0:T(8,128)(2,1)S(1)} %shard_map.156), channel_id=1, replica_groups=mesh['y'=4,'zh'=2,'c'=2,'zl'=2,'x'=4] {'y','zh','zl','x'}, dimensions={0} | all-to-all | bytes 1310720 | tf_op jit(solution)/shard_map/all_to_all | solution.py:591
  48.8 0.1 shard_map.157
  49.0 16.9 %all_to_all.11.a_ref = bf16[64,40,128]{2,1,0:T(8,128)(2,1)S(1)} all-to-all(bf16[64,40,128]{2,1,0:T(8,128)(2,1)S(1)} %shard_map.157), channel_id=1, replica_groups=mesh['y'=4,'zh'=2,'c'=2,'zl'=2,'x'=4] {'y','zh','zl','x'}, dimensions={0} | all-to-all | bytes 1310720 | tf_op jit(solution)/shard_map/all_to_all | solution.py:599
  65.9 3.1 %collective-permute-start.4 = (bf16[64,40,128]{2,1,0:T(8,128)(2,1)S(1)}, bf16[64,40,128]{2,1,0:T(8,128)(2,1)S(1)}, u32[]{:S(2)}, u32[]{:S(2)}) collective-permute-start(bf16[64,40,128]{2,1,0:T(8,128)(2,1)S(1)} %all_to_all.11.a_ref), channel_id=1, source_target_pairs={{0,8},{8,0},{1,9},{9,1},{2,10},{10,2},{3,11},{11,3},{4,12},{12,4},... | collective-permute-start | bytes 1966088 | tf_op jit(solution)/shard_map/ppermute | solution.py:600
  69.0 1.7 %collective-permute-done.4.b_ref = bf16[64,40,128]{2,1,0:T(8,128)(2,1)S(1)} collective-permute-done((bf16[64,40,128]{2,1,0:T(8,128)(2,1)S(1)}, bf16[64,40,128]{2,1,0:T(8,128)(2,1)S(1)}, u32[]{:S(2)}, u32[]{:S(2)}) %collective-permute-start.4) | collective-permute-done | bytes 655392 | tf_op jit(solution)/shard_map/ppermute | solution.py:600
  70.7 1.7 %shard_map.158 = (bf16[2,6,48,192]{3,2,1,0:T(8,128)(2,1)}, f32[1,192]{1,0:T(1,128)}, f32[192,576]{1,0:T(8,128)}, f32[192,192]{1,0:T(8,128)}, f32[1,192]{1,0:T(1,...) custom-call(bf16[64,40,128]{2,1,0:T(8,128)(2,1)S(1)} %all_to_all.11.a_ref, ...), custom_call_target="tpu_custom_call" | custom-call | tf_op jit(solution)/shard_map/pallas_call | solution.py:603
  (6 shorter events, 0.0 us)
Async XLA Ops:
  0.6 12.1 %copy-start.5 = (f32[192]{0:T(256)S(1)}, f32[192]{0:T(256)}, u32[]{:S(2)}) copy-start(f32[192]{0:T(256)} %param.14) | copy-start | bytes 2308
  0.6 12.1 %copy-start.6 = (f32[192]{0:T(256)S(1)}, f32[192]{0:T(256)}, u32[]{:S(2)}) copy-start(f32[192]{0:T(256)} %param.11) | copy-start | bytes 2308
  0.7 12.2 %copy-start.4 = (f32[1,6,3312]{2,0,1:T(1,128)S(1)}, f32[1,6,3312]{2,0,1:T(1,128)}, u32[]{:S(2)}) copy-start(f32[1,6,3312]{2,0,1:T(1,128)} %param.17) | copy-start | bytes 238468
  0.7 12.3 %copy-start.1 = (bf16[768,192]{0,1:T(8,128)(2,1)S(1)}, bf16[768,192]{0,1:T(8,128)(2,1)}, u32[]{:S(2)}) copy-start(bf16[768,192]{0,1:T(8,128)(2,1)} %param.16) | copy-start | bytes 884740
  0.7 12.3 %copy-start = (bf16[192,768]{1,0:T(8,128)(2,1)S(1)}, bf16[192,768]{1,0:T(8,128)(2,1)}, u32[]{:S(2)}) copy-start(bf16[192,768]{1,0:T(8,128)(2,1)} %param.15) | copy-start | bytes 884740
  0.7 12.3 %copy-start.3 = (bf16[192,192]{1,0:T(8,128)(2,1)S(1)}, bf16[192,192]{1,0:T(8,128)(2,1)}, u32[]{:S(2)}) copy-start(bf16[192,192]{1,0:T(8,128)(2,1)} %param.13) | copy-start | bytes 221188
  0.7 12.3 %copy-start.2 = (bf16[192,576]{1,0:T(8,128)(2,1)S(1)}, bf16[192,576]{1,0:T(8,128)(2,1)}, u32[]{:S(2)}) copy-start(bf16[192,576]{1,0:T(8,128)(2,1)} %param.12) | copy-start | bytes 663556
  2.1 12.4 %collective-permute-start.1 = (bf16[2,3,3,6,128]{4,3,2,1,0:T(8,128)(2,1)S(1)}, bf16[2,3,3,6,128]{4,3,2,1,0:T(8,128)(2,1)S(1)}, u32[]{:S(2)}, u32[]{:S(2)}) collective-permute-start(bf16[2,3,3,6,128]{4,3,2,1,0:T(8,128)(2,1)S(1)} %get-tuple-element.30), channel_id=1, source_target_pairs={{0,120},{8,0},{16,8},{24,16},{32,24},{40,32},{48,40},{56,48},{64,5... | collective-permute-start | bytes 82952 | tf_op jit(solution)/shard_map/ppermute | solution.py:571
  3.5 10.9 %collective-permute-start.2 = (bf16[2,3,3,6,128]{4,3,2,1,0:T(8,128)(2,1)S(1)}, bf16[2,3,3,6,128]{4,3,2,1,0:T(8,128)(2,1)S(1)}, u32[]{:S(2)}, u32[]{:S(2)}) collective-permute-start(bf16[2,3,3,6,128]{4,3,2,1,0:T(8,128)(2,1)S(1)} %get-tuple-element.31), channel_id=1, source_target_pairs={{0,127},{1,120},{2,121},{3,122},{4,123},{5,124},{6,125},{7,126},{8... | collective-permute-start | bytes 82952 | tf_op jit(solution)/shard_map/ppermute | solution.py:572
  12.2 6.3 %collective-permute-start = (bf16[2,3,128,128]{3,2,1,0:T(8,128)(2,1)S(1)}, bf16[2,3,128,128]{3,2,1,0:T(8,128)(2,1)S(1)}, u32[]{:S(2)}, u32[]{:S(2)}) collective-permute-start(bf16[2,3,128,128]{3,2,1,0:T(8,128)(2,1)S(1)} %get-tuple-element.29), channel_id=1, source_target_pairs={{0,7},{1,0},{2,1},{3,2},{4,3},{5,4},{6,5},{7,6},{8,15},{9,8},{10,9... | collective-permute-start | bytes 589832 | tf_op jit(solution)/shard_map/ppermute | solution.py:570
  27.0 2.6 %collective-permute-start.3 = (bf16[64,32,128]{2,1,0:T(8,128)(2,1)S(1)}, bf16[64,32,128]{2,1,0:T(8,128)(2,1)S(1)}, u32[]{:S(2)}, u32[]{:S(2)}) collective-permute-start(bf16[64,32,128]{2,1,0:T(8,128)(2,1)S(1)} %get-tuple-element.35), channel_id=1, source_target_pairs={{0,8},{8,0},{1,9},{9,1},{2,10},{10,2},{3,11},{11,3},{4,12},{12,4},... | collective-permute-start | bytes 1572872 | tf_op jit(solution)/shard_map/ppermute | solution.py:581
  65.9 4.8 %collective-permute-start.4 = (bf16[64,40,128]{2,1,0:T(8,128)(2,1)S(1)}, bf16[64,40,128]{2,1,0:T(8,128)(2,1)S(1)}, u32[]{:S(2)}, u32[]{:S(2)}) collective-permute-start(bf16[64,40,128]{2,1,0:T(8,128)(2,1)S(1)} %all_to_all.11.a_ref), channel_id=1, source_target_pairs={{0,8},{8,0},{1,9},{9,1},{2,10},{10,2},{3,11},{11,3},{4,12},{12,4},... | collective-permute-start | bytes 1966088 | tf_op jit(solution)/shard_map/ppermute | solution.py:600
